TPU v7x, 128 devices: a whole 4x4x4 slice. The times are simulated.
128 devices in a mesh: rows: 4 (over x), cols: 32 (over z, y, core).
Axes of the slice: x: 4, y: 4, z: 4, core: 2. Of those that a mesh axis runs over, the one named last changes fastest.
Arguments:
- values: bfloat16 [2, 2048, 262144], P(None, 'rows', 'cols'), may hold values from -0.01171875 to 0.01171875
- block_ids: int32 [2, 4, 32, 64], P(None, 'rows', 'cols'), may hold values from -1 to 1023, as said below
- labels: int32 [2, 2048], P(None, 'rows'), may hold values from 0 to 1
- table: float32 [1024, 128, 128], P('cols'), may hold values from -3 to 3
- table_acc: float32 [1024, 128, 128], P('cols'), may hold values from 1e-05 to 0.001
- lin: float32 [1024, 128], P('cols'), may hold values from -3 to 3
- lin_acc: float32 [1024, 128], P('cols'), may hold values from 1e-05 to 0.001
Outputs:
- new_table: float32 [1024, 128, 128], P('cols')
- new_lin: float32 [1024, 128], P('cols')
- logits: float32 [2, 2048], P(None, 'rows')
Inputs may be any that keep to these rules, and one draw needn't show every extreme that they name: `block_ids`: each list holds its active ids first and -1 after them; active ids of one list are distinct; at most 4 active ids of one list lie in one owner range (id // 32); a list has 48 to 64 active ids and some list has 64; in each minibatch one owner range, drawn from the seed, gets exactly 4 ids from every list.
All inputs are finite; a program needn't handle non-finite values.
Results may differ from a plain program's by a relative error of at most 0.0049.
Values may be sent and summed in bfloat16 or wider, within the bound.
A program may use at most 128 MiB of HBM per device.

v0:
```python
import jax
import jax.numpy as jnp
from jax import lax
from jax.sharding import PartitionSpec as P

learn_rate = 0.2


def list_slots(block_list, blocks_dev, owners, per_owner):
    listed = block_list.shape[0]
    present = block_list >= 0
    owner_of = jnp.where(present, block_list // blocks_dev, -1)
    same_owner = (owner_of[:, None] == owner_of[None, :]) & present[:, None]
    before = jnp.arange(listed)[None, :] < jnp.arange(listed)[:, None]
    rank_in = jnp.sum((same_owner & before).astype(jnp.int32), axis=1)
    slot_of = jnp.where(present, owner_of * per_owner + rank_in, -1)
    hits = slot_of[:, None] == jnp.arange(owners * per_owner)[None, :]
    holder = jnp.sum(jnp.where(hits, jnp.arange(listed)[:, None] + 1, 0), axis=0) - 1
    wanted = jnp.sum(jnp.where(hits, (block_list % blocks_dev)[:, None] + 1, 0), axis=0) - 1
    return (present, slot_of, holder, wanted)


def adagrad(weights, accum, grads):
    accum = accum + grads * grads
    return (weights - learn_rate * grads / jnp.sqrt(accum), accum)


def local(values, block_ids, labels, table, table_acc, lin, lin_acc):
    owners = lax.axis_size("cols")
    listed = block_ids.shape[3]
    per_owner = 2 * listed // owners
    slot_count = owners * per_owner
    blocks_dev, width, factors = table.shape
    logit_list = []
    for step in range(values.shape[0]):
        block_list = block_ids[step, 0, 0]
        present, slot_of, holder, wanted = list_slots(block_list, blocks_dev, owners, per_owner)
        asked = lax.all_to_all(
            wanted.reshape(owners, per_owner), "cols", split_axis=0, concat_axis=0, tiled=True
        )
        have = asked >= 0
        safe = jnp.where(have, asked, 0)
        sent_tiles = jnp.where(have[:, :, None, None], table[safe], 0.0).astype(jnp.bfloat16)
        sent_lin = jnp.where(have[:, :, None], lin[safe], 0.0).astype(jnp.bfloat16)
        got_tiles, got_lin = (
            lax.all_to_all(sent_tiles, "cols", split_axis=0, concat_axis=0, tiled=True),
            lax.all_to_all(sent_lin, "cols", split_axis=0, concat_axis=0, tiled=True),
        )
        pick = jnp.where(present, slot_of, 0)
        factor_rows = got_tiles.reshape(slot_count, width, factors)[pick].reshape(
            listed * width, factors
        )
        linear_rows = got_lin.reshape(slot_count, width)[pick].reshape(listed * width)
        mask = jnp.repeat(present, width)
        active = jnp.where(mask[None, :], values[step], jnp.zeros((), jnp.bfloat16))
        xv_part = jnp.dot(active, factor_rows, preferred_element_type=jnp.float32)
        factor_float = factor_rows.astype(jnp.float32)
        sumsq = jnp.sum(factor_float * factor_float, axis=1)
        active_float = active.astype(jnp.float32)
        sq_part = jnp.sum(active_float * active_float * sumsq[None, :], axis=1)
        lin_part = jnp.dot(active, linear_rows, preferred_element_type=jnp.float32)
        label_rows = labels[step].astype(jnp.float32)
        xv_sum, sq_sum, lin_sum = lax.psum((xv_part, sq_part, lin_part), "cols")
        logit = lin_sum + 0.5 * (jnp.sum(xv_sum * xv_sum, axis=1) - sq_sum)
        slope = jax.nn.sigmoid(logit) - label_rows
        weighted = (slope[:, None] * xv_sum).astype(jnp.bfloat16)
        grad_factor = lax.dot_general(
            active, weighted, (((0,), (0,)), ((), ())), preferred_element_type=jnp.float32
        )
        weight_sq = jnp.sum(active_float * active_float * slope[:, None], axis=0)
        grad_factor = grad_factor - factor_float * weight_sq[:, None]
        grad_linear = jnp.sum(active_float * slope[:, None], axis=0)
        tile_grad = grad_factor.astype(jnp.bfloat16).reshape(listed, width, factors)
        lin_grad = grad_linear.astype(jnp.bfloat16).reshape(listed, width)
        filled = holder >= 0
        source = jnp.where(filled, holder, 0)
        push_tiles = jnp.where(
            filled[:, None, None], tile_grad[source], jnp.zeros((), jnp.bfloat16)
        )
        push_lin = jnp.where(filled[:, None], lin_grad[source], jnp.zeros((), jnp.bfloat16))
        arrived, arrived_lin = (
            lax.all_to_all(
                push_tiles.reshape(owners, per_owner, width, factors),
                "cols",
                split_axis=0,
                concat_axis=0,
                tiled=True,
            ),
            lax.all_to_all(
                push_lin.reshape(owners, per_owner, width),
                "cols",
                split_axis=0,
                concat_axis=0,
                tiled=True,
            ),
        )
        onehot = (asked.reshape(slot_count)[:, None] == jnp.arange(blocks_dev)[None, :]).astype(
            jnp.bfloat16
        )
        dense = lax.dot_general(
            onehot,
            arrived.reshape(slot_count, width * factors),
            (((0,), (0,)), ((), ())),
            preferred_element_type=jnp.float32,
        ).reshape(blocks_dev, width, factors)
        dense_lin = lax.dot_general(
            onehot,
            arrived_lin.reshape(slot_count, width),
            (((0,), (0,)), ((), ())),
            preferred_element_type=jnp.float32,
        )
        grad_table, grad_lin = lax.psum((dense, dense_lin), "rows")
        table, table_acc = adagrad(table, table_acc, grad_table)
        lin, lin_acc = adagrad(lin, lin_acc, grad_lin)
        logit_list.append(logit)
    return (table, lin, jnp.stack(logit_list))


def solution(mesh):
    in_specs = (
        P(None, "rows", "cols"),
        P(None, "rows", "cols", None),
        P(None, "rows"),
        P("cols", None, None),
        P("cols", None, None),
        P("cols", None),
        P("cols", None),
    )
    out_specs = (P("cols", None, None), P("cols", None), P(None, "rows"))
    return jax.shard_map(local, mesh=mesh, in_specs=in_specs, out_specs=out_specs, check_vma=False)
```

profile of v0, /device:TPU:1, one launch (start us, length us, event | category | flops | bytes accessed | tf_op | source)
XLA Modules:
  0.0 729.0 jit_solution(7636514985591731445)
XLA Ops:
  11.0 16.3 %all_to_all.58 = s32[32,1,4]{2,1,0:T(1,128)S(1)} all-to-all(s32[32,1,4]{2,1,0:T(1,128)S(1)} %bitcast.218), channel_id=1, replica_groups=mesh['rows'=4,'cols'=32] {'cols'}, dimensions={0} | all-to-all | bytes 1024 | tf_op jit(solution)/shard_map/all_to_all | solution.py:38
  43.5 7.7 %all-to-all-start.2 = ((bf16[32,4,128,128]{3,2,1,0:T(8,128)(2,1)}), bf16[32,4,128,128]{3,2,1,0:T(8,128)(2,1)}, u32[]{:S(2)}, u32[]{:S(2)}) async-start(bf16[32,4,128,128]{3,2,1,0:T(8,128)(2,1)} %select_convert_fusion.1), calls=%async_computation.2 | async-start | bytes 8388608 | tf_op jit(solution)/shard_map/all_to_all | solution.py:46
  57.9 43.6 %all-to-all-done.2 = bf16[32,4,128,128]{3,2,1,0:T(8,128)(2,1)} async-done(((bf16[32,4,128,128]{3,2,1,0:T(8,128)(2,1)}), bf16[32,4,128,128]{3,2,1,0:T(8,128)(2,1)}, u32[]{:S(2)}, u32[]{:S(2)}) %all-to-all-start.2) | async-done | bytes 4194336 | tf_op jit(solution)/shard_map/all_to_all | solution.py:46
  119.0 65.8 %all-reduce.1 = (f32[512]{0:T(512)S(1)}, f32[512]{0:T(512)S(1)}) all-reduce(f32[512]{0:T(512)S(1)} %bitcast.224, f32[512]{0:T(512)S(1)} %fusion.6), channel_id=1, replica_groups=mesh['rows'=4,'cols'=32] {'cols'}, use_global_device_ids=true, to_apply=%region_3.4 | all-reduce | flops 1024 | bytes 8192 | tf_op jit(solution)/shard_map/psum | solution.py:63
  184.8 28.8 %all-reduce.7.cloned.1.call-done = f32[512,128]{1,0:T(8,128)} async-done(((f32[512,128]{1,0:T(8,128)}), f32[512,128]{1,0:T(8,128)}) %all-reduce.7.cloned.1.call-update) | async-done | bytes 262160 | tf_op jit(solution)/shard_map/psum | solution.py:63
  221.4 6.8 fusion.10
  244.6 48.9 %all-to-all-done.3 = bf16[32,4,128,128]{3,2,1,0:T(8,128)(2,1)} async-done(((bf16[32,4,128,128]{3,2,1,0:T(8,128)(2,1)}), bf16[32,4,128,128]{3,2,1,0:T(8,128)(2,1)}, u32[]{:S(2)}, u32[]{:S(2)}) %all-to-all-start.3) | async-done | bytes 4194336 | tf_op jit(solution)/shard_map/all_to_all | solution.py:82
  293.5 7.7 %copy.111 = bf16[16,8,128,128]{3,1,2,0:T(8,128)(2,1)} copy(bf16[16,8,128,128]{3,2,1,0:T(8,128)(2,1)} %bitcast.62) | data formatting | bytes 8388608
  312.9 13.2 %all_to_all.59 = s32[32,1,4]{2,1,0:T(1,128)S(1)} all-to-all(s32[32,1,4]{2,1,0:T(1,128)S(1)} %bitcast.219), channel_id=1, replica_groups=mesh['rows'=4,'cols'=32] {'cols'}, dimensions={0} | all-to-all | bytes 1024 | tf_op jit(solution)/shard_map/all_to_all | solution.py:38
  332.1 7.2 all-to-all-done.5
  339.5 13.1 %psum.74 = f32[32,128]{1,0:T(8,128)S(1)} all-reduce(f32[32,128]{1,0:T(8,128)S(1)} %fusion.30), channel_id=1, replica_groups=mesh['rows'=4,'cols'=32] {'rows'}, use_global_device_ids=true, to_apply=%region_15.16 | all-reduce | flops 4096 | bytes 32768 | tf_op jit(solution)/shard_map/psum | solution.py:112
  354.0 17.1 %all-to-all-start.6 = ((bf16[32,4,128]{2,1,0:T(4,128)(2,1)}), bf16[32,4,128]{2,1,0:T(4,128)(2,1)S(1)}, u32[]{:S(2)}, u32[]{:S(2)}) async-start(bf16[32,4,128]{2,1,0:T(4,128)(2,1)} %select_convert_fusion.2), calls=%async_computation.6 | async-start | bytes 65536 | tf_op jit(solution)/shard_map/all_to_all | solution.py:47
  384.4 7.7 %all-to-all-start.7 = ((bf16[32,4,128,128]{3,2,1,0:T(8,128)(2,1)}), bf16[32,4,128,128]{3,2,1,0:T(8,128)(2,1)}, u32[]{:S(2)}, u32[]{:S(2)}) async-start(bf16[32,4,128,128]{3,2,1,0:T(8,128)(2,1)} %select_convert_fusion), calls=%async_computation.7 | async-start | bytes 8388608 | tf_op jit(solution)/shard_map/all_to_all | solution.py:46
  398.7 43.7 %all-to-all-done.7 = bf16[32,4,128,128]{3,2,1,0:T(8,128)(2,1)} async-done(((bf16[32,4,128,128]{3,2,1,0:T(8,128)(2,1)}), bf16[32,4,128,128]{3,2,1,0:T(8,128)(2,1)}, u32[]{:S(2)}, u32[]{:S(2)}) %all-to-all-start.7) | async-done | bytes 4194336 | tf_op jit(solution)/shard_map/all_to_all | solution.py:46
  449.5 7.0 fusion.12
  463.2 65.8 %all-reduce = (f32[512]{0:T(512)S(1)}, f32[512]{0:T(512)S(1)}) all-reduce(f32[512]{0:T(512)S(1)} %bitcast.225, f32[512]{0:T(512)S(1)} %fusion.4), channel_id=1, replica_groups=mesh['rows'=4,'cols'=32] {'cols'}, use_global_device_ids=true, to_apply=%region_16.17 | all-reduce | flops 1024 | bytes 8192 | tf_op jit(solution)/shard_map/psum | solution.py:63
  529.0 27.4 %all-reduce.11.cloned.1.call-done = f32[512,128]{1,0:T(8,128)} async-done(((f32[512,128]{1,0:T(8,128)}), f32[512,128]{1,0:T(8,128)}) %all-reduce.11.cloned.1.call-update) | async-done | bytes 262160 | tf_op jit(solution)/shard_map/psum | solution.py:63
  557.5 6.8 fusion.9
  564.3 6.9 fusion.11
  587.0 49.4 %all-to-all-done.8 = bf16[32,4,128,128]{3,2,1,0:T(8,128)(2,1)} async-done(((bf16[32,4,128,128]{3,2,1,0:T(8,128)(2,1)}), bf16[32,4,128,128]{3,2,1,0:T(8,128)(2,1)}, u32[]{:S(2)}, u32[]{:S(2)}) %all-to-all-start.8) | async-done | bytes 4194336 | tf_op jit(solution)/shard_map/all_to_all | solution.py:82
  636.4 7.7 %copy.110 = bf16[16,8,128,128]{3,1,2,0:T(8,128)(2,1)} copy(bf16[16,8,128,128]{3,2,1,0:T(8,128)(2,1)} %bitcast.66) | data formatting | bytes 8388608
  657.0 7.0 all-to-all-start.9
  671.5 14.5 %psum.79 = f32[32,128]{1,0:T(8,128)S(1)} all-reduce(f32[32,128]{1,0:T(8,128)S(1)} %fusion.28), channel_id=1, replica_groups=mesh['rows'=4,'cols'=32] {'rows'}, use_global_device_ids=true, to_apply=%region_25.26 | all-reduce | flops 4096 | bytes 32768 | tf_op jit(solution)/shard_map/psum | solution.py:112
  686.6 27.5 %all-reduce.13.cloned.1.call-done = f32[32,128,128]{2,0,1:T(8,128)} async-done(((f32[32,128,128]{2,0,1:T(8,128)}), f32[32,128,128]{2,0,1:T(8,128)}) %all-reduce.13.cloned.1.call-update) | async-done | bytes 2097168 | tf_op jit(solution)/shard_map/psum | solution.py:112
  (124 shorter events, 166.8 us)
Async XLA Ops:
  29.8 13.7 %all-to-all-start.1 = ((bf16[32,4,128]{2,1,0:T(4,128)(2,1)}), bf16[32,4,128]{2,1,0:T(4,128)(2,1)S(1)}, u32[]{:S(2)}, u32[]{:S(2)}) async-start(bf16[32,4,128]{2,1,0:T(4,128)(2,1)} %select_convert_fusion.3), calls=%async_computation.1 | async-start | bytes 65536 | tf_op jit(solution)/shard_map/all_to_all | solution.py:47
  43.5 7.9 %copy-start.6 = (s32[2,1,1,64]{3,2,1,0:T(1,128)S(1)}, s32[2,1,1,64]{3,2,1,0:T(1,128)}, u32[]{:S(2)}) copy-start(s32[2,1,1,64]{3,2,1,0:T(1,128)} %param.8) | copy-start | bytes 1540
  43.5 8.0 %copy-start.7 = (s32[2,512]{1,0:T(2,128)S(1)}, s32[2,512]{1,0:T(2,128)}, u32[]{:S(2)}) copy-start(s32[2,512]{1,0:T(2,128)} %param.9) | copy-start | bytes 12292
  43.5 58.0 %all-to-all-start.2 = ((bf16[32,4,128,128]{3,2,1,0:T(8,128)(2,1)}), bf16[32,4,128,128]{3,2,1,0:T(8,128)(2,1)}, u32[]{:S(2)}, u32[]{:S(2)}) async-start(bf16[32,4,128,128]{3,2,1,0:T(8,128)(2,1)} %select_convert_fusion.1), calls=%async_computation.2 | async-start | bytes 8388608 | tf_op jit(solution)/shard_map/all_to_all | solution.py:46
  51.2 162.4 %all-reduce.7.cloned.1.call-start = ((), (), s32[]{:S(2)}) async-start(), calls=%async_computation.10 | async-start | bytes 524288 | tf_op jit(solution)/shard_map/psum | solution.py:63
  214.7 6.7 copy-start.4
  237.4 56.2 %all-to-all-start.3 = ((bf16[32,4,128,128]{3,2,1,0:T(8,128)(2,1)}), bf16[32,4,128,128]{3,2,1,0:T(8,128)(2,1)}, u32[]{:S(2)}, u32[]{:S(2)}) async-start(bf16[32,4,128,128]{3,2,1,0:T(8,128)(2,1)} %broadcast_select_fusion.7), calls=%async_computation.3 | async-start | bytes 8388608 | tf_op jit(solution)/shard_map/all_to_all | solution.py:82
  243.3 128.0 %all-reduce.9.cloned.1.call-start = ((), (), s32[]{:S(2)}) async-start(), calls=%async_computation.11 | async-start | bytes 4194304 | tf_op jit(solution)/shard_map/psum | solution.py:112
  307.6 44.9 %copy-start.2 = (f32[32,128]{1,0:T(8,128)S(1)}, f32[32,128]{1,0:T(8,128)}, u32[]{:S(2)}) copy-start(f32[32,128]{1,0:T(8,128)} %param.12) | copy-start | bytes 49156
  307.6 44.9 %copy-start.5 = (f32[32,128]{1,0:T(8,128)S(1)}, f32[32,128]{1,0:T(8,128)}, u32[]{:S(2)}) copy-start(f32[32,128]{1,0:T(8,128)} %param.13) | copy-start | bytes 49156
  307.6 63.6 %copy-start = (f32[32,128,128]{2,1,0:T(8,128)S(1)}, f32[32,128,128]{2,1,0:T(8,128)}, u32[]{:S(2)}) copy-start(f32[32,128,128]{2,1,0:T(8,128)} %param.10) | copy-start | bytes 6291460
  327.8 11.5 %all-to-all-start.5 = ((bf16[32,4,128]{2,1,0:T(4,128)(2,1)}), bf16[32,4,128]{2,1,0:T(4,128)(2,1)S(1)}, u32[]{:S(2)}, u32[]{:S(2)}) async-start(bf16[32,4,128]{2,1,0:T(4,128)(2,1)} %broadcast_select_fusion.9), calls=%async_computation.5 | async-start | bytes 65536 | tf_op jit(solution)/shard_map/all_to_all | solution.py:89
  354.0 30.4 %all-to-all-start.6 = ((bf16[32,4,128]{2,1,0:T(4,128)(2,1)}), bf16[32,4,128]{2,1,0:T(4,128)(2,1)S(1)}, u32[]{:S(2)}, u32[]{:S(2)}) async-start(bf16[32,4,128]{2,1,0:T(4,128)(2,1)} %select_convert_fusion.2), calls=%async_computation.6 | async-start | bytes 65536 | tf_op jit(solution)/shard_map/all_to_all | solution.py:47
  384.4 58.0 %all-to-all-start.7 = ((bf16[32,4,128,128]{3,2,1,0:T(8,128)(2,1)}), bf16[32,4,128,128]{3,2,1,0:T(8,128)(2,1)}, u32[]{:S(2)}, u32[]{:S(2)}) async-start(bf16[32,4,128,128]{3,2,1,0:T(8,128)(2,1)} %select_convert_fusion), calls=%async_computation.7 | async-start | bytes 8388608 | tf_op jit(solution)/shard_map/all_to_all | solution.py:46
  392.1 164.2 %all-reduce.11.cloned.1.call-start = ((), (), s32[]{:S(2)}) async-start(), calls=%async_computation.12 | async-start | bytes 524288 | tf_op jit(solution)/shard_map/psum | solution.py:63
  557.5 6.8 copy-start.1
  557.5 6.8 copy-start.3
  580.3 56.2 %all-to-all-start.8 = ((bf16[32,4,128,128]{3,2,1,0:T(8,128)(2,1)}), bf16[32,4,128,128]{3,2,1,0:T(8,128)(2,1)}, u32[]{:S(2)}, u32[]{:S(2)}) async-start(bf16[32,4,128,128]{3,2,1,0:T(8,128)(2,1)} %broadcast_select_fusion.6), calls=%async_computation.8 | async-start | bytes 8388608 | tf_op jit(solution)/shard_map/all_to_all | solution.py:82
  586.2 127.9 %all-reduce.13.cloned.1.call-start = ((), (), s32[]{:S(2)}) async-start(), calls=%async_computation.13 | async-start | bytes 4194304 | tf_op jit(solution)/shard_map/psum | solution.py:112
  657.0 14.4 %all-to-all-start.9 = ((bf16[32,4,128]{2,1,0:T(4,128)(2,1)}), bf16[32,4,128]{2,1,0:T(4,128)(2,1)S(1)}, u32[]{:S(2)}, u32[]{:S(2)}) async-start(bf16[32,4,128]{2,1,0:T(4,128)(2,1)} %broadcast_select_fusion.8), calls=%async_computation.9 | async-start | bytes 65536 | tf_op jit(solution)/shard_map/all_to_all | solution.py:89
Sparse Core Ops, SparseCore 0:
  112.4 101.1 all-reduce.6
  312.9 58.2 all-reduce.8
  456.6 99.6 all-reduce.10
  655.7 58.4 all-reduce.12
where the time goes:
time: 739 us; the launch traced here: 729 us
  waiting for transfers between devices  284 us (38%)
  blocking collectives  189 us (26%)
  other arithmetic  71.4 us (10%)
  local copies, waits for them, and re-layouts  62.2 us (8%)
  starting transfers between devices  59.8 us (8%)
  matrix products  48.8 us (7%)
  between operations  14.6 us (2%)
    psum x2, blocking collectives, local(): xv_sum, sq_sum, lin_sum = lax.psum((xv_part, sq_part, lin_part), 'cols')  132 us
    all_to_all x2, waiting for transfers between devices, local(): lax.all_to_all(push_tiles.reshape(owners, per_owner, width, factors), 'co...  98.3 us
    all_to_all x2, waiting for transfers between devices, local(): lax.all_to_all(sent_tiles, 'cols', split_axis=0, concat_axis=0, tiled=True)  87.3 us
    psum x2, waiting for transfers between devices, local(): xv_sum, sq_sum, lin_sum = lax.psum((xv_part, sq_part, lin_part), 'cols')  56.2 us
    all_to_all x2, blocking collectives, local(): lax.all_to_all(wanted.reshape(owners, per_owner), 'cols', split_axis=0, c...  29.5 us
    psum x2, waiting for transfers between devices, local(): grad_table, grad_lin = lax.psum((dense, dense_lin), 'rows')  27.7 us
    psum x2, blocking collectives, local(): grad_table, grad_lin = lax.psum((dense, dense_lin), 'rows')  27.5 us
    all_to_all x2, starting transfers between devices, local(): lax.all_to_all(sent_lin, 'cols', split_axis=0, concat_axis=0, tiled=True)  21.2 us
  transfers between devices with their start and end apart: 12, of which 10 were waited for; matrix products, arithmetic and copies ran while one was open for 8% of the time, Pallas kernels for 0%

commit v1 on v0

v1 whole, which is shorter than its diff:
```python
import jax
import jax.numpy as jnp
from jax import lax
from jax.experimental import pallas as pl
from jax.experimental.pallas import tpu as pltpu
from jax.sharding import PartitionSpec as P

MESH = pl.DeviceIdType.MESH
learn_rate = 0.2
ROWS, COLS, ZS, YS = 4, 32, 4, 4
PEERS = ROWS * COLS
SLOTS = 4
WIDTH = 128
EX = 512
PART = EX // COLS
BLOCKS = 32
STEPS = 2
F32, BF16, I32 = jnp.float32, jnp.bfloat16, jnp.int32


def nt(a, b):
    return lax.dot_general(a, b, (((1,), (1,)), ((), ())), preferred_element_type=F32)


def nn(a, b):
    return lax.dot_general(a, b, (((1,), (0,)), ((), ())), preferred_element_type=F32)


def iota(shape, dim):
    return lax.broadcasted_iota(I32, shape, dim)


def kernel(
    holder, wanted, label, table, table_acc, lin, lin_acc, values,
    delta_out, lin_out, logit_out,
    v0, v1, asks, ids_v, ids_s, keys, keys8, tab_f, acc_f, lin_f, lacc_f, tab_b, lin_b,
    pull, pull_lin, got, got_lin, stats, xs, xr, ws, wr, swt, gs, gls, rp, rl, dense, lin_part, lin_got, last,
    v_sem, ask_send, ask_recv, ids_sem, pull_send, pull_recv, plin_send, plin_recv, x_send, x_recv, w_send, w_recv,
    push_send, push_recv, glin_send, glin_recv, sum_send, sum_recv, out_send, out_recv,
):
    r, c = lax.axis_index("rows"), lax.axis_index("cols")
    z, y, k = c // 8, (c // 2) % 4, c % 2

    def offsets(d):
        dz = d % 4
        return dz, (d // 8 + dz) % 4, (d // 4) % 2

    def ahead(d):
        dz, dy, dk = offsets(d)
        return ((z + dz) % 4) * 8 + ((y + dy) % 4) * 2 + (k + dk) % 2

    def behind(d):
        dz, dy, dk = offsets(d)
        return ((z + 4 - dz) % 4) * 8 + ((y + 4 - dy) % 4) * 2 + (k + dk) % 2

    def send(src, dst, send_sem, recv_sem, row, col, home):
        @pl.when(home)
        def _():
            pltpu.make_async_copy(src, dst, recv_sem).start()

        @pl.when(jnp.logical_not(home))
        def _():
            pltpu.make_async_remote_copy(
                src_ref=src, dst_ref=dst, send_sem=send_sem, recv_sem=recv_sem,
                device_id=(row, col), device_id_type=MESH,
            ).start()

    def landed(ref, sem):
        pltpu.make_async_copy(ref, ref, sem).wait()

    for t in range(STEPS):
        v = (v0, v1)[t]

        def bring(j, _):
            columns = pl.ds(pl.multiple_of(j * WIDTH, WIDTH), WIDTH)
            pltpu.make_async_copy(values.at[t, :, columns], v.at[j], v_sem.at[t]).start()
            return 0

        lax.fori_loop(0, 64, bring, 0)

    def ask(d, _):
        tr, tc = (r + d // COLS) % ROWS, ahead(d % COLS)
        send(wanted.at[tc], asks.at[r * COLS + c], ask_send, ask_recv, tr, tc, d == 0)
        return 0

    lax.fori_loop(0, PEERS, ask, 0)

    tab_f[...] = table[...]
    acc_f[...] = table_acc[...]
    lin_f[...] = lin[...]
    lacc_f[...] = lin_acc[...]
    tab_b[0] = jnp.zeros((16, 256), BF16)
    tab_b[pl.ds(1, BLOCKS)] = table[...].astype(BF16).reshape(BLOCKS, 16, 256)
    lin_b[0] = jnp.zeros((1, WIDTH), F32)
    lin_b[pl.ds(1, BLOCKS)] = lin[...].reshape(BLOCKS, 1, WIDTH)

    landed(asks, ask_recv)
    ids = jnp.sum(asks[...].reshape(ROWS, COLS, STEPS, WIDTH), axis=1).reshape(ROWS * STEPS, WIDTH)
    ids_v[...] = ids
    to_scalar = pltpu.make_async_copy(ids_v, ids_s, ids_sem)
    to_scalar.start()
    ids_b = ids.astype(F32).astype(BF16)
    for part in range(4):
        lane = iota((WIDTH, 512), 1) + part * 512
        spread = (iota((WIDTH, 512), 0) == lane // 16).astype(F32).astype(BF16)
        found = nn(ids_b, spread).astype(I32)
        keys[:, part * 512 : (part + 1) * 512] = (found - 1) * 16 + iota((8, 512), 1) % 16
    lane = iota((WIDTH, 256), 1)
    spread = ((iota((WIDTH, 256), 0) == (lane // 8) * 4 + lane % 8) & (lane % 8 < 4)).astype(F32).astype(BF16)
    keys8[...] = nn(ids_b, spread).astype(I32) - 1
    to_scalar.wait()
    landed(asks.at[pl.ds(0, PEERS - 1)], ask_send)

    for t in range(STEPS):
        if t > 0:
            landed(pull.at[pl.ds(0, PEERS - 1)], pull_send)
            landed(pull_lin.at[pl.ds(0, COLS - 1)], plin_send)

        def give(d, _):
            tc = ahead(d)
            for q in range(ROWS):
                tr = (r + q) % ROWS
                place = tr * COLS + tc
                for i in range(SLOTS):
                    pull[place, i] = tab_b[ids_s[tr * STEPS + t, tc * SLOTS + i]]
                send(
                    pull.at[place], got.at[t, c, r], pull_send, pull_recv.at[t, d],
                    tr, tc, (d == 0) & (q == 0),
                )
            return 0

        lax.fori_loop(0, COLS, give, 0)

        def give_lin(d, _):
            tc = ahead(d)
            for i in range(SLOTS):
                pull_lin[tc, pl.ds(i, 1)] = lin_b[ids_s[r * STEPS + t, tc * SLOTS + i]]
            pull_lin[tc, pl.ds(4, 4)] = jnp.zeros((4, WIDTH), F32)
            send(pull_lin.at[tc], got_lin.at[t, c], plin_send, plin_recv.at[t], r, tc, d == 0)
            return 0

        lax.fori_loop(0, COLS, give_lin, 0)

        v = (v0, v1)[t]
        landed(v, v_sem.at[t])
        stats[...] = jnp.zeros_like(stats)
        landed(got_lin.at[t], plin_recv.at[t])

        def block_of(o, i):
            return v[holder[t, o * SLOTS + i]]

        def tile_of(o, i):
            quarters = [got[t, o, q, i] for q in range(ROWS)]
            return jnp.concatenate(
                [quarters[q][:, h * WIDTH : (h + 1) * WIDTH] for q in range(ROWS) for h in range(2)], axis=0
            )

        def use(d, _):
            o = behind(d)
            landed(got.at[t, o], pull_recv.at[t, d])
            total = None
            for i in range(SLOTS):
                block = block_of(o, i)
                tile = tile_of(o, i)
                row = got_lin[t, o, pl.ds(i, 1)].astype(BF16).astype(F32)
                lin_rows = jnp.where(iota((WIDTH, WIDTH), 0) == 0, row, 0.0).astype(BF16)
                left = jnp.concatenate([block, block * block], axis=1)
                right = jnp.concatenate(
                    [
                        jnp.concatenate([tile, jnp.zeros((WIDTH, WIDTH), BF16)], axis=1),
                        jnp.concatenate([lin_rows, tile * tile * jnp.asarray(-0.5, BF16)], axis=1),
                    ],
                    axis=0,
                )
                part = nt(left, right)
                total = part if total is None else total + part
            stats[...] += total
            return 0

        lax.fori_loop(0, COLS, use, 0)

        if t > 0:
            landed(xs.at[pl.ds(0, COLS - 1)], x_send)
            landed(wr.at[t, pl.ds(0, COLS - 1)], w_send)
        xs[:, pl.ds(0, PART)] = stats[:, :WIDTH].reshape(COLS, PART, WIDTH)
        rest = jnp.sum(stats[:, WIDTH:], axis=1, keepdims=True)
        spot = iota((EX, WIDTH), 1) == iota((EX, WIDTH), 0) % PART
        rest = jnp.where(spot, rest, 0.0).reshape(COLS, 2, 8, WIDTH)
        xs[:, pl.ds(PART, 8)] = rest[:, 0] + rest[:, 1]

        def give_x(d, _):
            tc = ahead(d)
            send(xs.at[tc], xr.at[t, c], x_send, x_recv.at[t], r, tc, d == 0)
            return 0

        lax.fori_loop(0, COLS, give_x, 0)
        landed(xr.at[t], x_recv.at[t])
        summed = jnp.sum(xr[t], axis=0)
        xv = summed[:PART]
        rest = summed[PART : PART + 8]
        first = jnp.where(iota((8, WIDTH), 1) < 8, rest, 0.0)
        second = jnp.where(iota((8, WIDTH), 1) >= 8, rest, 0.0)
        rest = jnp.sum(jnp.concatenate([first, second], axis=0), axis=1, keepdims=True)
        logit = jnp.broadcast_to(rest + 0.5 * jnp.sum(xv * xv, axis=1, keepdims=True), (PART, WIDTH))
        slope = 1.0 / (1.0 + jnp.exp(-logit)) - label[t]
        weighted = (slope * xv).astype(BF16)

        def low(a):
            return a - a.astype(BF16).astype(F32)

        lane = iota((PART, WIDTH), 1)
        logit_low = low(logit)
        extra = jnp.where(
            lane < 64,
            jnp.where(lane < 32, slope, low(slope)),
            jnp.where(lane < 96, logit, jnp.where(lane < 112, logit_low, low(logit_low))),
        ).astype(BF16)
        ws[:, :WIDTH] = weighted
        ws[:, WIDTH:] = extra

        def give_w(d, _):
            tc = ahead(d)
            send(ws, wr.at[t, c], w_send, w_recv.at[t], r, tc, d == 0)
            return 0

        lax.fori_loop(0, COLS, give_w, 0)
        landed(wr.at[t], w_recv.at[t])
        turned = wr[t].reshape(EX, 2 * WIDTH).astype(F32).T
        swt[...] = turned.astype(BF16)
        logit_out[pl.ds(t, 1)] = turned[192:193] + turned[224:225] + turned[240:241]

        if t > 0:
            landed(gs.at[pl.ds(0, PEERS - 1)], push_send)
            landed(gls.at[pl.ds(0, COLS - 1)], glin_send)

        def grads(d, _):
            o = ahead(d)
            dz, _, _ = offsets(d)
            lins = []
            for i in range(SLOTS):
                block = block_of(o, i)
                right = jnp.concatenate([block, block * block], axis=1)
                res = nn(swt[...], right)
                both = res[WIDTH : WIDTH + 1] + res[WIDTH + 32 : WIDTH + 33]
                lins.append(both[:, :WIDTH])
                tile = res[:WIDTH, :WIDTH] - tile_of(o, i).astype(F32) * both[:, WIDTH:]
                tile = tile.astype(BF16)
                for q in range(ROWS):
                    for h in range(2):
                        at = 32 * q + 16 * h
                        gs[q * COLS + o, i, :, pl.ds(h * WIDTH, WIDTH)] = tile[at : at + 16]
            gls[o] = jnp.concatenate(lins + [jnp.zeros((4, WIDTH), F32)], axis=0)
            send(gls.at[o], rl.at[t, c], glin_send, glin_recv.at[t], r, o, d == 0)
            for dq in range(ROWS):
                q = (r + dq) % ROWS
                send(
                    gs.at[q * COLS + o], rp.at[t, r * COLS + c], push_send, push_recv.at[t, dz * 4 + dq],
                    q, o, (d == 0) & (dq == 0),
                )
            return 0

        lax.fori_loop(0, COLS, grads, 0)

        landed(rl.at[t], glin_recv.at[t])
        keyed = jnp.broadcast_to(keys8[pl.ds(r * STEPS + t, 1)], (BLOCKS, 256))
        onehot = (iota((BLOCKS, 256), 0) == keyed).astype(F32).astype(BF16)
        if t > 0:
            landed(lin_got.at[t, pl.ds(0, ROWS - 1)], sum_send)
        lin_part[...] = nn(onehot, rl[t].reshape(COLS * 8, WIDTH).astype(BF16))
        for dq in range(ROWS):
            q = (r + dq) % ROWS
            send(lin_part, lin_got.at[t, r], sum_send, sum_recv.at[t], q, c, dq == 0)

        dense[...] = jnp.zeros_like(dense)

        def add(n, _):
            dz, dq = n // 4, n % 4
            rs, zs = (r + 4 - dq) % 4, (z + 4 - dz) % 4
            at = rs * COLS + zs * 8
            landed(rp.at[t, pl.ds(at, 8)], push_recv.at[t, n])
            keyed = keys[pl.ds(rs * STEPS + t, 1), pl.ds(pl.multiple_of(zs * 512, 512), 512)]
            onehot = (iota((512, 512), 0) == jnp.broadcast_to(keyed, (512, 512))).astype(F32).astype(BF16)
            dense[...] += nn(onehot, rp[t, pl.ds(at, 8)].reshape(512, 256))
            return 0

        lax.fori_loop(0, 16, add, 0)

        grad = dense[...]
        acc = acc_f[...] + grad * grad
        acc_f[...] = acc
        new = tab_f[...] - learn_rate * grad / jnp.sqrt(acc)
        tab_f[...] = new
        if t < STEPS - 1:
            tab_b[pl.ds(1, BLOCKS)] = new.astype(BF16).reshape(BLOCKS, 16, 256)
        else:
            last[...] = (table[...] - new).astype(BF16)
            for dq in range(ROWS):
                q = (r + dq) % ROWS
                send(last, delta_out.at[r], out_send, out_recv, q, c, dq == 0)

        landed(lin_got.at[t], sum_recv.at[t])
        grad = lin_got[t, 0] + lin_got[t, 1] + lin_got[t, 2] + lin_got[t, 3]
        acc = lacc_f[...] + grad * grad
        lacc_f[...] = acc
        new = lin_f[...] - learn_rate * grad / jnp.sqrt(acc)
        lin_f[...] = new
        lin_b[pl.ds(1, BLOCKS)] = new.reshape(BLOCKS, 1, WIDTH)

    lin_out[...] = lin_f[...]
    landed(pull.at[pl.ds(0, PEERS - 1)], pull_send)
    landed(pull_lin.at[pl.ds(0, COLS - 1)], plin_send)
    landed(xs.at[pl.ds(0, COLS - 1)], x_send)
    landed(wr.at[0, pl.ds(0, COLS - 1)], w_send)
    landed(gs.at[pl.ds(0, PEERS - 1)], push_send)
    landed(gls.at[pl.ds(0, COLS - 1)], glin_send)
    landed(lin_got.at[0, pl.ds(0, ROWS - 1)], sum_send)
    landed(delta_out, out_recv)
    landed(delta_out.at[pl.ds(0, ROWS - 1)], out_send)


def list_slots(lists):
    listed = lists.shape[1]
    present = lists >= 0
    owner = jnp.where(present, lists // BLOCKS, -1)
    before = jnp.arange(listed)[None, :] < jnp.arange(listed)[:, None]
    same = (owner[:, :, None] == owner[:, None, :]) & before[None]
    rank = jnp.sum(same.astype(I32), axis=2)
    slot = jnp.where(present, owner * SLOTS + rank, -1)
    hits = slot[:, :, None] == jnp.arange(COLS * SLOTS)[None, None, :]
    holder = jnp.sum(jnp.where(hits, jnp.arange(listed)[None, :, None], 0), axis=1)
    wanted = jnp.sum(jnp.where(hits, (lists % BLOCKS)[:, :, None] + 1, 0), axis=1)
    return holder, wanted


def local(values, block_ids, labels, table, table_acc, lin, lin_acc):
    r, c = lax.axis_index("rows"), lax.axis_index("cols")
    holder, wanted = list_slots(block_ids[:, 0, 0])
    mine = (jnp.arange(WIDTH) // SLOTS == c)[None, None, :]
    wanted = jnp.tile(wanted.reshape(STEPS, COLS, SLOTS), (1, 1, COLS))
    wanted = jnp.where(mine, wanted, 0).transpose(1, 0, 2)
    label = lax.dynamic_slice_in_dim(labels, c * PART, PART, axis=1).astype(F32)
    label = jnp.broadcast_to(label[:, :, None], (STEPS, PART, WIDTH))

    def quarter(a):
        a = lax.dynamic_slice_in_dim(a, r * 32, 32, axis=2)
        a = a.reshape(BLOCKS, WIDTH, 2, 16).transpose(0, 3, 2, 1)
        return a.reshape(BLOCKS * 16, 256)

    vmem = pl.BlockSpec(memory_space=pltpu.VMEM)
    hbm = pl.BlockSpec(memory_space=pl.ANY)
    dma, V = pltpu.SemaphoreType.DMA, pltpu.VMEM
    delta, new_lin, logits = pl.pallas_call(
        kernel,
        out_shape=(
            jax.ShapeDtypeStruct((ROWS, BLOCKS * 16, 256), BF16),
            jax.ShapeDtypeStruct((BLOCKS, WIDTH), F32),
            jax.ShapeDtypeStruct((STEPS, EX), F32),
        ),
        in_specs=[pl.BlockSpec(memory_space=pltpu.SMEM)] + [vmem] * 6 + [hbm],
        out_specs=(hbm, vmem, vmem),
        scratch_shapes=[
            V((64, EX, WIDTH), BF16),
            V((64, EX, WIDTH), BF16),
            V((PEERS, STEPS, WIDTH), I32),
            V((8, WIDTH), I32),
            pltpu.SMEM((8, WIDTH), I32),
            V((8, 2048), I32),
            V((8, 256), I32),
            V((512, 256), F32),
            V((512, 256), F32),
            V((BLOCKS, WIDTH), F32),
            V((BLOCKS, WIDTH), F32),
            V((BLOCKS + 1, 16, 256), BF16),
            V((BLOCKS + 1, 1, WIDTH), F32),
            V((PEERS, SLOTS, 16, 256), BF16),
            V((COLS, 8, WIDTH), F32),
            V((STEPS, COLS, ROWS, SLOTS, 16, 256), BF16),
            V((STEPS, COLS, 8, WIDTH), F32),
            V((EX, 256), F32),
            V((COLS, 24, WIDTH), F32),
            V((STEPS, COLS, 24, WIDTH), F32),
            V((PART, 256), BF16),
            V((STEPS, COLS, PART, 256), BF16),
            V((256, EX), BF16),
            V((PEERS, SLOTS, 16, 256), BF16),
            V((COLS, 8, WIDTH), F32),
            V((STEPS, PEERS, SLOTS, 16, 256), BF16),
            V((STEPS, COLS, 8, WIDTH), F32),
            V((512, 256), F32),
            V((BLOCKS, WIDTH), F32),
            V((STEPS, ROWS, BLOCKS, WIDTH), F32),
            V((512, 256), BF16),
            dma((STEPS,)),
            dma, dma, dma,
            dma, dma((STEPS, COLS)),
            dma, dma((STEPS,)),
            dma, dma((STEPS,)),
            dma, dma((STEPS,)),
            dma, dma((STEPS, 16)),
            dma, dma((STEPS,)),
            dma, dma((STEPS,)),
            dma, dma,
        ],
        compiler_params=pltpu.CompilerParams(has_side_effects=True, vmem_limit_bytes=60 * 2**20),
    )(holder, wanted, label, quarter(table), quarter(table_acc), lin, lin_acc, values)
    delta = delta.reshape(ROWS, BLOCKS, 16, 2, WIDTH).transpose(1, 4, 0, 3, 2).reshape(table.shape)
    return table - delta.astype(F32), new_lin, logits


def solution(mesh):
    in_specs = (
        P(None, "rows", "cols"),
        P(None, "rows", "cols", None),
        P(None, "rows"),
        P("cols", None, None),
        P("cols", None, None),
        P("cols", None),
        P("cols", None),
    )
    out_specs = (P("cols", None, None), P("cols", None), P(None, "rows"))
    return jax.shard_map(local, mesh=mesh, in_specs=in_specs, out_specs=out_specs, check_vma=False)
```

time: 739 us -> 350 us (0.47); the launches traced: 729 us -> 350 us
  Pallas kernels: 0 us -> 324 us
  waiting for transfers between devices: 284 us -> 0 us
  blocking collectives: 189 us -> 0 us
  other arithmetic: 71.4 us -> 5.42 us
  starting transfers between devices: 59.8 us -> 0 us
  matrix products: 48.8 us -> 0 us
  local copies, waits for them, and re-layouts: 62.2 us -> 20.1 us
  between operations: 14.6 us -> 0.73 us
    pallas_call x0 -> x1, Pallas kernels: none -> 324 us  [local(): pl.pallas_call(kernel, out_shape=(jax.ShapeDtypeStruct((ROWS, BLOCKS * 16...]
    all_to_all x8 -> x0, waiting for transfers between devices: 200 us -> none  [the longest x2 98.3 us: local(): lax.all_to_all(push_tiles.reshape(owners, per_owner, width, factors), 'co...]
    psum x4 -> x0, blocking collectives: 159 us -> none  [the longest x2 132 us: local(): xv_sum, sq_sum, lin_sum = lax.psum((xv_part, sq_part, lin_part), 'cols')]
    psum x4 -> x0, waiting for transfers between devices: 83.9 us -> none  [the longest x2 56.2 us: local(): xv_sum, sq_sum, lin_sum = lax.psum((xv_part, sq_part, lin_part), 'cols')]
    all_to_all x8 -> x0, starting transfers between devices: 59.6 us -> none  [the longest x2 21.2 us: local(): lax.all_to_all(sent_lin, 'cols', split_axis=0, concat_axis=0, tiled=True)]
    dot_general x10 -> x0, matrix products: 48.8 us -> none  [the longest x2 13.7 us: local(): lax.dot_general(active, weighted, (((0,), (0,)), ((), ())), preferred_ele...]
    reduce_sum x10 -> x2, other arithmetic: 33.3 us -> 0.86 us  [the longest x1 0.68 us: list_slots(): jnp.sum(jnp.where(hits, (lists % BLOCKS)[:, :, None] + 1, 0), axis=1)]
    all_to_all x2 -> x0, blocking collectives: 29.5 us -> none  [local(): lax.all_to_all(wanted.reshape(owners, per_owner), 'cols', split_axis=0, c...]
  transfers between devices with their start and end apart: 12 -> 0, of which waited for: 10 -> 0; matrix products, arithmetic and copies ran while one was open for 8% -> 0% of each run, Pallas kernels for 0% -> 0%
where the time goes in v1:
time: 350 us
  Pallas kernels  324 us (93%)
  local copies, waits for them, and re-layouts  20.1 us (6%)
  other arithmetic  5.42 us (2%)
    pallas_call x1, Pallas kernels, local(): pl.pallas_call(kernel, out_shape=(jax.ShapeDtypeStruct((ROWS, BLOCKS * 16...  324 us
    unnamed x13, local copies, waits for them, and re-layouts  9.41 us

profile of v1, /device:TPU:1, one launch (start us, length us, event | category | flops | bytes accessed | tf_op | source)
XLA Modules:
  0.0 349.9 jit_solution(12000529583198555362)
XLA Ops:
  0.7 0.9 dynamic-slice_convert_fusion
  1.6 0.7 fusion.1
  2.3 0.2 convert_reduce_fusion
  2.4 0.7 add_select_fusion
  3.1 0.7 select_reduce_fusion
  3.8 0.7 broadcast_in_dim.58.label
  4.5 0.1 tile.10
  4.6 0.1 copy.20
  4.8 0.6 select_bitcast_fusion.wanted
  5.4 2.9 copy.27
  8.3 1.1 constant_dynamic-slice_fusion
  9.4 0.3 copy.23
  9.7 2.0 constant_dynamic-slice_fusion.1
  11.6 2.2 copy.29
  13.8 0.3 copy.25
  14.1 1.1 copy_bitcast_fusion
  15.1 323.7 %shard_map.94 = (bf16[4,512,256]{2,1,0:T(8,128)(2,1)}, f32[32,128]{1,0:T(8,128)}, f32[2,512]{1,0:T(2,128)}) custom-call(s32[2,128]{1,0:T(2,128)} %get-tuple-element.16.holder, s32[32,2,128]{2,1,0:T(2,128)} %select_bitcast_fusion.wanted, f32[2,16,128]{2,1,0:T(8,128)} %broadcast_in_dim.58.label, f32[512,256]{1,0:T(8,128)} %get-tuple-element.20.table, ...), custom_call_target="tpu_custom_call" | custom-call | tf_op jit(solution)/shard_map/pallas_call | solution.py:352
  338.9 3.1 reshape.165
  342.0 1.9 copy.26
  343.9 0.3 copy-done.1
  344.2 1.6 bitcast_subtract_fusion
  345.8 2.9 copy.28
  348.7 0.6 copy.36
  349.3 0.6 copy.37
  (11 shorter events, 0.1 us)
Async XLA Ops:
  0.6 9.0 %copy-start = (f32[32,128,128]{2,1,0:T(8,128)S(1)}, f32[32,128,128]{2,1,0:T(8,128)}, u32[]{:S(2)}) copy-start(f32[32,128,128]{2,1,0:T(8,128)} %param.11) | copy-start | bytes 6291460
  342.0 2.2 copy-start.1
  345.8 2.9 copy-start.2
  345.8 3.5 %copy-start.3 = (f32[2,512]{1,0:T(2,128)S(1)}, f32[2,512]{1,0:T(2,128)}, u32[]{:S(2)}) copy-start(f32[2,512]{1,0:T(2,128)} %get-tuple-element.26) | copy-start | bytes 12292

commit v2 on v1

--- a/solution.py
+++ b/solution.py
@@ -31,11 +31,11 @@
 
 
 def kernel(
-    holder, wanted, label, table, table_acc, lin, lin_acc, values,
+    holder, wanted, labels, lin, lin_acc, table, table_acc, values,
     delta_out, lin_out, logit_out,
-    v0, v1, asks, ids_v, ids_s, keys, keys8, tab_f, acc_f, lin_f, lacc_f, tab_b, lin_b,
-    pull, pull_lin, got, got_lin, stats, xs, xr, ws, wr, swt, gs, gls, rp, rl, dense, lin_part, lin_got, last,
-    v_sem, ask_send, ask_recv, ids_sem, pull_send, pull_recv, plin_send, plin_recv, x_send, x_recv, w_send, w_recv,
+    v0, v1, tab_n, acc_n, asks, rows_ids, ids_v, ids_s, keys, keys8, tab_f, tab_0, acc_f, lin_f, lacc_f, tab_b, lin_b,
+    pull, pull_lin, got, got_lin, stats, xs, xr, ws, wr, swt, gs, gls, rp, rl, dense, lin_part, lin_got, last, back,
+    v_sem, tab_sem, acc_sem, ask_send, ask_recv, row_send, row_recv, ids_sem, pull_send, pull_recv, plin_send, plin_recv, x_send, x_recv, w_send, w_recv,
     push_send, push_recv, glin_send, glin_recv, sum_send, sum_recv, out_send, out_recv,
 ):
     r, c = lax.axis_index("rows"), lax.axis_index("cols")
@@ -68,6 +68,18 @@
     def landed(ref, sem):
         pltpu.make_async_copy(ref, ref, sem).wait()
 
+    bring_tab = pltpu.make_async_copy(table, tab_n, tab_sem)
+    bring_acc = pltpu.make_async_copy(table_acc, acc_n, acc_sem)
+    bring_tab.start()
+    bring_acc.start()
+
+    def ask(d, _):
+        tc = ahead(d)
+        send(wanted.at[tc], asks.at[c], ask_send, ask_recv, r, tc, d == 0)
+        return 0
+
+    lax.fori_loop(0, COLS, ask, 0)
+
     for t in range(STEPS):
         v = (v0, v1)[t]
 
@@ -78,38 +90,62 @@
 
         lax.fori_loop(0, 64, bring, 0)
 
-    def ask(d, _):
-        tr, tc = (r + d // COLS) % ROWS, ahead(d % COLS)
-        send(wanted.at[tc], asks.at[r * COLS + c], ask_send, ask_recv, tr, tc, d == 0)
-        return 0
-
-    lax.fori_loop(0, PEERS, ask, 0)
-
-    tab_f[...] = table[...]
-    acc_f[...] = table_acc[...]
     lin_f[...] = lin[...]
     lacc_f[...] = lin_acc[...]
     tab_b[0] = jnp.zeros((16, 256), BF16)
-    tab_b[pl.ds(1, BLOCKS)] = table[...].astype(BF16).reshape(BLOCKS, 16, 256)
     lin_b[0] = jnp.zeros((1, WIDTH), F32)
     lin_b[pl.ds(1, BLOCKS)] = lin[...].reshape(BLOCKS, 1, WIDTH)
 
+    def quarter(src, dst):
+        pick = (iota((32, WIDTH), 1) == iota((32, WIDTH), 0) + 32 * r).astype(F32).astype(BF16)
+
+        def turn(n, _):
+            rest = src[pl.ds(n * 4, 4)].reshape(4 * WIDTH, WIDTH)
+            total = None
+            for _ in range(3):
+                piece = rest.astype(BF16)
+                rest = rest - piece.astype(F32)
+                part = nt(pick, piece)
+                total = part if total is None else total + part
+            for i in range(4):
+                for h in range(2):
+                    dst[pl.ds(pl.multiple_of(n * 64 + i * 16, 16), 16), h * WIDTH : (h + 1) * WIDTH] = total[
+                        h * 16 : (h + 1) * 16, i * WIDTH : (i + 1) * WIDTH
+                    ]
+            return 0
+
+        lax.fori_loop(0, BLOCKS // 4, turn, 0)
+
+    bring_tab.wait()
+    quarter(tab_n, tab_0)
+    tab_f[...] = tab_0[...]
+    tab_b[pl.ds(1, BLOCKS)] = tab_0[...].astype(BF16).reshape(BLOCKS, 16, 256)
+
     landed(asks, ask_recv)
-    ids = jnp.sum(asks[...].reshape(ROWS, COLS, STEPS, WIDTH), axis=1).reshape(ROWS * STEPS, WIDTH)
+    rows_ids[r] = jnp.sum(asks[...], axis=0)
+    for dq in range(1, ROWS):
+        pltpu.make_async_remote_copy(
+            src_ref=rows_ids.at[r], dst_ref=rows_ids.at[r], send_sem=row_send, recv_sem=row_recv.at[dq],
+            device_id=((r + dq) % ROWS, c), device_id_type=MESH,
+        ).start()
+    for dq in range(1, ROWS):
+        landed(rows_ids.at[(r + 4 - dq) % ROWS], row_recv.at[dq])
+    ids = rows_ids[...].reshape(ROWS * STEPS, WIDTH)
     ids_v[...] = ids
     to_scalar = pltpu.make_async_copy(ids_v, ids_s, ids_sem)
     to_scalar.start()
     ids_b = ids.astype(F32).astype(BF16)
     for part in range(4):
         lane = iota((WIDTH, 512), 1) + part * 512
-        spread = (iota((WIDTH, 512), 0) == lane // 16).astype(F32).astype(BF16)
+        spread = (iota((WIDTH, 512), 0) == behind(lane // 64) * 4 + (lane // 16) % 4).astype(F32).astype(BF16)
         found = nn(ids_b, spread).astype(I32)
         keys[:, part * 512 : (part + 1) * 512] = (found - 1) * 16 + iota((8, 512), 1) % 16
     lane = iota((WIDTH, 256), 1)
     spread = ((iota((WIDTH, 256), 0) == (lane // 8) * 4 + lane % 8) & (lane % 8 < 4)).astype(F32).astype(BF16)
     keys8[...] = nn(ids_b, spread).astype(I32) - 1
     to_scalar.wait()
-    landed(asks.at[pl.ds(0, PEERS - 1)], ask_send)
+    landed(asks.at[pl.ds(0, COLS - 1)], ask_send)
+    landed(rows_ids.at[pl.ds(0, ROWS - 1)], row_send)
 
     for t in range(STEPS):
         if t > 0:
@@ -118,6 +154,10 @@
 
         def give(d, _):
             tc = ahead(d)
+            for i in range(SLOTS):
+                pull_lin[tc, pl.ds(i, 1)] = lin_b[ids_s[r * STEPS + t, tc * SLOTS + i]]
+            pull_lin[tc, pl.ds(4, 4)] = jnp.zeros((4, WIDTH), F32)
+            send(pull_lin.at[tc], got_lin.at[t, c], plin_send, plin_recv.at[t, d], r, tc, d == 0)
             for q in range(ROWS):
                 tr = (r + q) % ROWS
                 place = tr * COLS + tc
@@ -131,20 +171,12 @@
 
         lax.fori_loop(0, COLS, give, 0)
 
-        def give_lin(d, _):
-            tc = ahead(d)
-            for i in range(SLOTS):
-                pull_lin[tc, pl.ds(i, 1)] = lin_b[ids_s[r * STEPS + t, tc * SLOTS + i]]
-            pull_lin[tc, pl.ds(4, 4)] = jnp.zeros((4, WIDTH), F32)
-            send(pull_lin.at[tc], got_lin.at[t, c], plin_send, plin_recv.at[t], r, tc, d == 0)
-            return 0
-
-        lax.fori_loop(0, COLS, give_lin, 0)
-
         v = (v0, v1)[t]
+        if t == 0:
+            bring_acc.wait()
+            quarter(acc_n, acc_f)
         landed(v, v_sem.at[t])
         stats[...] = jnp.zeros_like(stats)
-        landed(got_lin.at[t], plin_recv.at[t])
 
         def block_of(o, i):
             return v[holder[t, o * SLOTS + i]]
@@ -157,24 +189,19 @@
 
         def use(d, _):
             o = behind(d)
+            landed(got_lin.at[t, o], plin_recv.at[t, d])
             landed(got.at[t, o], pull_recv.at[t, d])
-            total = None
+            blocks = [block_of(o, i) for i in range(SLOTS)]
+            tiles = [tile_of(o, i) for i in range(SLOTS)]
+            stats[:, :WIDTH] += nt(jnp.concatenate(blocks, axis=1), jnp.concatenate(tiles, axis=1))
+            rest = None
             for i in range(SLOTS):
-                block = block_of(o, i)
-                tile = tile_of(o, i)
+                block, tile = blocks[i].astype(F32), tiles[i].astype(F32)
+                square = -0.5 * jnp.sum(tile * tile, axis=0, keepdims=True)
                 row = got_lin[t, o, pl.ds(i, 1)].astype(BF16).astype(F32)
-                lin_rows = jnp.where(iota((WIDTH, WIDTH), 0) == 0, row, 0.0).astype(BF16)
-                left = jnp.concatenate([block, block * block], axis=1)
-                right = jnp.concatenate(
-                    [
-                        jnp.concatenate([tile, jnp.zeros((WIDTH, WIDTH), BF16)], axis=1),
-                        jnp.concatenate([lin_rows, tile * tile * jnp.asarray(-0.5, BF16)], axis=1),
-                    ],
-                    axis=0,
-                )
-                part = nt(left, right)
-                total = part if total is None else total + part
-            stats[...] += total
+                part = block * (block * square + row)
+                rest = part if rest is None else rest + part
+            stats[:, WIDTH:] += rest
             return 0
 
         lax.fori_loop(0, COLS, use, 0)
@@ -202,7 +229,10 @@
         second = jnp.where(iota((8, WIDTH), 1) >= 8, rest, 0.0)
         rest = jnp.sum(jnp.concatenate([first, second], axis=0), axis=1, keepdims=True)
         logit = jnp.broadcast_to(rest + 0.5 * jnp.sum(xv * xv, axis=1, keepdims=True), (PART, WIDTH))
-        slope = 1.0 / (1.0 + jnp.exp(-logit)) - label[t]
+        row = labels[pl.ds(t, 1), pl.ds(pl.multiple_of((c // 8) * WIDTH, WIDTH), WIDTH)].astype(F32)
+        mine = iota((PART, WIDTH), 1) == iota((PART, WIDTH), 0) + (c % 8) * PART
+        label = jnp.sum(jnp.where(mine, row, 0.0), axis=1, keepdims=True)
+        slope = 1.0 / (1.0 + jnp.exp(-logit)) - label
         weighted = (slope * xv).astype(BF16)
 
         def low(a):
@@ -235,7 +265,6 @@
 
         def grads(d, _):
             o = ahead(d)
-            dz, _, _ = offsets(d)
             lins = []
             for i in range(SLOTS):
                 block = block_of(o, i)
@@ -254,13 +283,26 @@
             for dq in range(ROWS):
                 q = (r + dq) % ROWS
                 send(
-                    gs.at[q * COLS + o], rp.at[t, r * COLS + c], push_send, push_recv.at[t, dz * 4 + dq],
+                    gs.at[q * COLS + o], rp.at[t, dq * COLS + d], push_send, push_recv.at[t, (d // 4) * 4 + dq],
                     q, o, (d == 0) & (dq == 0),
                 )
             return 0
 
         lax.fori_loop(0, COLS, grads, 0)
 
+        dense[...] = jnp.zeros_like(dense)
+
+        def add(n, _):
+            g, dq = n // 4, n % 4
+            rs = (r + 4 - dq) % 4
+            at = dq * COLS + g * 4
+            landed(rp.at[t, pl.ds(at, 4)], push_recv.at[t, n])
+            keyed = keys[pl.ds(rs * STEPS + t, 1), pl.ds(pl.multiple_of(g * 256, 256), 256)]
+            onehot = (iota((512, 256), 0) == jnp.broadcast_to(keyed, (512, 256))).astype(F32).astype(BF16)
+            dense[...] += nn(onehot, rp[t, pl.ds(at, 4)].reshape(256, 256))
+            return 0
+
+        lax.fori_loop(0, 28, add, 0)
         landed(rl.at[t], glin_recv.at[t])
         keyed = jnp.broadcast_to(keys8[pl.ds(r * STEPS + t, 1)], (BLOCKS, 256))
         onehot = (iota((BLOCKS, 256), 0) == keyed).astype(F32).astype(BF16)
@@ -271,19 +313,7 @@
             q = (r + dq) % ROWS
             send(lin_part, lin_got.at[t, r], sum_send, sum_recv.at[t], q, c, dq == 0)
 
-        dense[...] = jnp.zeros_like(dense)
-
-        def add(n, _):
-            dz, dq = n // 4, n % 4
-            rs, zs = (r + 4 - dq) % 4, (z + 4 - dz) % 4
-            at = rs * COLS + zs * 8
-            landed(rp.at[t, pl.ds(at, 8)], push_recv.at[t, n])
-            keyed = keys[pl.ds(rs * STEPS + t, 1), pl.ds(pl.multiple_of(zs * 512, 512), 512)]
-            onehot = (iota((512, 512), 0) == jnp.broadcast_to(keyed, (512, 512))).astype(F32).astype(BF16)
-            dense[...] += nn(onehot, rp[t, pl.ds(at, 8)].reshape(512, 256))
-            return 0
-
-        lax.fori_loop(0, 16, add, 0)
+        lax.fori_loop(28, 32, add, 0)
 
         grad = dense[...]
         acc = acc_f[...] + grad * grad
@@ -293,10 +323,10 @@
         if t < STEPS - 1:
             tab_b[pl.ds(1, BLOCKS)] = new.astype(BF16).reshape(BLOCKS, 16, 256)
         else:
-            last[...] = (table[...] - new).astype(BF16)
+            last[...] = (tab_0[...] - new).astype(BF16)
             for dq in range(ROWS):
                 q = (r + dq) % ROWS
-                send(last, delta_out.at[r], out_send, out_recv, q, c, dq == 0)
+                send(last, back.at[r], out_send, out_recv, q, c, dq == 0)
 
         landed(lin_got.at[t], sum_recv.at[t])
         grad = lin_got[t, 0] + lin_got[t, 1] + lin_got[t, 2] + lin_got[t, 3]
@@ -314,8 +344,19 @@
     landed(gs.at[pl.ds(0, PEERS - 1)], push_send)
     landed(gls.at[pl.ds(0, COLS - 1)], glin_send)
     landed(lin_got.at[0, pl.ds(0, ROWS - 1)], sum_send)
-    landed(delta_out, out_recv)
-    landed(delta_out.at[pl.ds(0, ROWS - 1)], out_send)
+    landed(back, out_recv)
+    eye = (iota((WIDTH, WIDTH), 0) == iota((WIDTH, WIDTH), 1)).astype(F32).astype(BF16)
+
+    def back_turn(b, _):
+        at = pl.ds(pl.multiple_of(b * 16, 16), 16)
+        tile = jnp.concatenate(
+            [back[q, at, h * WIDTH : (h + 1) * WIDTH] for q in range(ROWS) for h in range(2)], axis=0
+        )
+        delta_out[b] = nt(eye, tile).astype(BF16)
+        return 0
+
+    lax.fori_loop(0, BLOCKS, back_turn, 0)
+    landed(back.at[pl.ds(0, ROWS - 1)], out_send)
 
 
 def list_slots(lists):
@@ -333,39 +374,35 @@
 
 
 def local(values, block_ids, labels, table, table_acc, lin, lin_acc):
-    r, c = lax.axis_index("rows"), lax.axis_index("cols")
+    c = lax.axis_index("cols")
     holder, wanted = list_slots(block_ids[:, 0, 0])
     mine = (jnp.arange(WIDTH) // SLOTS == c)[None, None, :]
     wanted = jnp.tile(wanted.reshape(STEPS, COLS, SLOTS), (1, 1, COLS))
     wanted = jnp.where(mine, wanted, 0).transpose(1, 0, 2)
-    label = lax.dynamic_slice_in_dim(labels, c * PART, PART, axis=1).astype(F32)
-    label = jnp.broadcast_to(label[:, :, None], (STEPS, PART, WIDTH))
-
-    def quarter(a):
-        a = lax.dynamic_slice_in_dim(a, r * 32, 32, axis=2)
-        a = a.reshape(BLOCKS, WIDTH, 2, 16).transpose(0, 3, 2, 1)
-        return a.reshape(BLOCKS * 16, 256)
-
     vmem = pl.BlockSpec(memory_space=pltpu.VMEM)
     hbm = pl.BlockSpec(memory_space=pl.ANY)
     dma, V = pltpu.SemaphoreType.DMA, pltpu.VMEM
     delta, new_lin, logits = pl.pallas_call(
         kernel,
         out_shape=(
-            jax.ShapeDtypeStruct((ROWS, BLOCKS * 16, 256), BF16),
+            jax.ShapeDtypeStruct((BLOCKS, WIDTH, WIDTH), BF16),
             jax.ShapeDtypeStruct((BLOCKS, WIDTH), F32),
             jax.ShapeDtypeStruct((STEPS, EX), F32),
         ),
-        in_specs=[pl.BlockSpec(memory_space=pltpu.SMEM)] + [vmem] * 6 + [hbm],
-        out_specs=(hbm, vmem, vmem),
+        in_specs=[pl.BlockSpec(memory_space=pltpu.SMEM)] + [vmem] * 4 + [hbm] * 3,
+        out_specs=(vmem, vmem, vmem),
         scratch_shapes=[
             V((64, EX, WIDTH), BF16),
             V((64, EX, WIDTH), BF16),
-            V((PEERS, STEPS, WIDTH), I32),
+            V((BLOCKS, WIDTH, WIDTH), F32),
+            V((BLOCKS, WIDTH, WIDTH), F32),
+            V((COLS, STEPS, WIDTH), I32),
+            V((ROWS, STEPS, WIDTH), I32),
             V((8, WIDTH), I32),
             pltpu.SMEM((8, WIDTH), I32),
             V((8, 2048), I32),
             V((8, 256), I32),
+            V((512, 256), F32),
             V((512, 256), F32),
             V((512, 256), F32),
             V((BLOCKS, WIDTH), F32),
@@ -390,20 +427,22 @@
             V((BLOCKS, WIDTH), F32),
             V((STEPS, ROWS, BLOCKS, WIDTH), F32),
             V((512, 256), BF16),
+            V((ROWS, 512, 256), BF16),
             dma((STEPS,)),
-            dma, dma, dma,
+            dma, dma,
+            dma, dma,
+            dma, dma((ROWS,)), dma,
+            dma, dma((STEPS, COLS)),
             dma, dma((STEPS, COLS)),
             dma, dma((STEPS,)),
             dma, dma((STEPS,)),
-            dma, dma((STEPS,)),
-            dma, dma((STEPS, 16)),
+            dma, dma((STEPS, 32)),
             dma, dma((STEPS,)),
             dma, dma((STEPS,)),
             dma, dma,
         ],
         compiler_params=pltpu.CompilerParams(has_side_effects=True, vmem_limit_bytes=60 * 2**20),
-    )(holder, wanted, label, quarter(table), quarter(table_acc), lin, lin_acc, values)
-    delta = delta.reshape(ROWS, BLOCKS, 16, 2, WIDTH).transpose(1, 4, 0, 3, 2).reshape(table.shape)
+    )(holder, wanted, labels, lin, lin_acc, table, table_acc, values)
     return table - delta.astype(F32), new_lin, logits
 
 

time: 350 us -> 298 us (0.85)
  Pallas kernels: 324 us -> 289 us
  local copies, waits for them, and re-layouts: 20.1 us -> 1.49 us
    pallas_call x1, Pallas kernels: 324 us -> 289 us  [local(): pl.pallas_call(kernel, out_shape=(jax.ShapeDtypeStruct((BLOCKS, WIDTH, WI...]
    unnamed x13 -> x8, local copies, waits for them, and re-layouts: 9.41 us -> 1.21 us
    convert_element_type x2 -> x0, local copies, waits for them, and re-layouts: 5.06 us -> none  [local(): return (table - delta.astype(F32), new_lin, logits)]
where the time goes in v2:
time: 298 us; the launch traced here: 297 us
  Pallas kernels  289 us (97%)
  other arithmetic  5.82 us (2%)
    pallas_call x1, Pallas kernels, local(): pl.pallas_call(kernel, out_shape=(jax.ShapeDtypeStruct((BLOCKS, WIDTH, WI...  289 us

profile of v2, /device:TPU:1, one launch (start us, length us, event | category | flops | bytes accessed | tf_op | source)
XLA Modules:
  0.0 297.3 jit_solution(1041061350759008014)
XLA Ops:
  0.6 0.7 fusion.1
  1.3 0.2 convert_reduce_fusion
  1.5 0.7 add_select_fusion
  2.2 0.7 select_reduce_fusion
  2.9 0.1 tile.10
  3.0 0.1 copy.12
  3.1 0.1 copy.13
  3.2 0.6 select_bitcast_fusion.wanted
  3.8 0.0 copy-start
  3.8 289.3 %shard_map.94 = (bf16[32,128,128]{2,1,0:T(8,128)(2,1)}, f32[32,128]{1,0:T(8,128)}, f32[2,512]{1,0:T(2,128)}) custom-call(s32[2,128]{1,0:T(2,128)} %get-tuple-element.10.holder, s32[32,2,128]{2,1,0:T(2,128)} %select_bitcast_fusion.wanted, s32[2,512]{1,0:T(2,128)} %labels.1, f32[32,128]{1,0:T(8,128)} %lin.1, f32[32,128]{1,0:T(8,128)} %lin_acc.1, ...), custom_call_target="tpu_custom_call" | custom-call | tf_op jit(solution)/shard_map/pallas_call | solution.py:385
  293.1 0.0 copy-done
  293.1 0.0 copy-start.1
  293.1 0.0 copy-start.2
  293.2 2.9 convert_subtract_fusion
  296.1 0.0 copy-done.1
  296.1 0.6 copy.16
  296.7 0.0 copy-done.2
  296.7 0.6 copy.17
  (3 shorter events, 0.0 us)
Async XLA Ops:
  3.8 289.3 %copy-start = (f32[32,128,128]{2,1,0:T(8,128)S(1)}, f32[32,128,128]{2,1,0:T(8,128)}, u32[]{:S(2)}) copy-start(f32[32,128,128]{2,1,0:T(8,128)} %table.1) | copy-start | bytes 6291460
  293.1 2.9 copy-start.1
  293.1 3.5 %copy-start.2 = (f32[2,512]{1,0:T(2,128)S(1)}, f32[2,512]{1,0:T(2,128)}, u32[]{:S(2)}) copy-start(f32[2,512]{1,0:T(2,128)} %get-tuple-element.18) | copy-start | bytes 12292

commit v3 on v2

--- a/solution.py
+++ b/solution.py
@@ -1,3 +1,5 @@
+import functools
+
 import jax
 import jax.numpy as jnp
 from jax import lax
@@ -33,9 +35,9 @@
 def kernel(
     holder, wanted, labels, lin, lin_acc, table, table_acc, values,
     delta_out, lin_out, logit_out,
-    v0, v1, tab_n, acc_n, asks, rows_ids, ids_v, ids_s, keys, keys8, tab_f, tab_0, acc_f, lin_f, lacc_f, tab_b, lin_b,
-    pull, pull_lin, got, got_lin, stats, xs, xr, ws, wr, swt, gs, gls, rp, rl, dense, lin_part, lin_got, last, back,
-    v_sem, tab_sem, acc_sem, ask_send, ask_recv, row_send, row_recv, ids_sem, pull_send, pull_recv, plin_send, plin_recv, x_send, x_recv, w_send, w_recv,
+    v0, v1, tab_n, acc_n, asks, rows_ids, ids_v, ids_s, mine_v, mine_s, keys, tab_all, tab_f, tab_0, acc_f, lin_f, lacc_f, tab_b, lin_b,
+    pull, pull_lin, got, got_lin, got_next, pull_next, stats, xs, xr, ws, wr, swt, gs, gls, rp, rl, dense, lin_part, lin_got, last, back,
+    v_sem, tab_sem, acc_sem, ask_send, ask_recv, mine_sem, row_send, row_recv, ids_sem, pull_send, next_send, pull_recv, plin_send, plin_recv, x_send, x_recv, w_send, w_recv,
     push_send, push_recv, glin_send, glin_recv, sum_send, sum_recv, out_send, out_recv,
 ):
     r, c = lax.axis_index("rows"), lax.axis_index("cols")
@@ -92,7 +94,8 @@
 
     lin_f[...] = lin[...]
     lacc_f[...] = lin_acc[...]
-    tab_b[0] = jnp.zeros((16, 256), BF16)
+    for h in range(2):
+        tab_b[h, 0] = jnp.zeros((16, WIDTH), BF16)
     lin_b[0] = jnp.zeros((1, WIDTH), F32)
     lin_b[pl.ds(1, BLOCKS)] = lin[...].reshape(BLOCKS, 1, WIDTH)
 
@@ -116,65 +119,94 @@
 
         lax.fori_loop(0, BLOCKS // 4, turn, 0)
 
+    eye = (iota((WIDTH, WIDTH), 0) == iota((WIDTH, WIDTH), 1)).astype(F32).astype(BF16)
+    tab_all[0] = jnp.zeros((ROWS, 16, 256), BF16)
     bring_tab.wait()
-    quarter(tab_n, tab_0)
-    tab_f[...] = tab_0[...]
-    tab_b[pl.ds(1, BLOCKS)] = tab_0[...].astype(BF16).reshape(BLOCKS, 16, 256)
+
+    def turn_all(n, _):
+        tiles = nt(eye, tab_n[pl.ds(n * 4, 4)].reshape(4 * WIDTH, WIDTH).astype(BF16)).astype(BF16)
+        for i in range(4):
+            for q in range(ROWS):
+                for h in range(2):
+                    at = 32 * q + 16 * h
+                    tab_all[n * 4 + i + 1, q, :, h * WIDTH : (h + 1) * WIDTH] = tiles[
+                        at : at + 16, i * WIDTH : (i + 1) * WIDTH
+                    ]
+        return 0
+
+    lax.fori_loop(0, BLOCKS // 4, turn_all, 0)
 
     landed(asks, ask_recv)
-    rows_ids[r] = jnp.sum(asks[...], axis=0)
+    own = jnp.sum(asks[...], axis=0)
+    mine_v[...] = own
+    rows_ids[r] = own
+    to_mine = pltpu.make_async_copy(mine_v, mine_s, mine_sem)
+    to_mine.start()
     for dq in range(1, ROWS):
         pltpu.make_async_remote_copy(
             src_ref=rows_ids.at[r], dst_ref=rows_ids.at[r], send_sem=row_send, recv_sem=row_recv.at[dq],
             device_id=((r + dq) % ROWS, c), device_id_type=MESH,
         ).start()
-    for dq in range(1, ROWS):
-        landed(rows_ids.at[(r + 4 - dq) % ROWS], row_recv.at[dq])
-    ids = rows_ids[...].reshape(ROWS * STEPS, WIDTH)
-    ids_v[...] = ids
-    to_scalar = pltpu.make_async_copy(ids_v, ids_s, ids_sem)
-    to_scalar.start()
-    ids_b = ids.astype(F32).astype(BF16)
-    for part in range(4):
-        lane = iota((WIDTH, 512), 1) + part * 512
-        spread = (iota((WIDTH, 512), 0) == behind(lane // 64) * 4 + (lane // 16) % 4).astype(F32).astype(BF16)
-        found = nn(ids_b, spread).astype(I32)
-        keys[:, part * 512 : (part + 1) * 512] = (found - 1) * 16 + iota((8, 512), 1) % 16
-    lane = iota((WIDTH, 256), 1)
-    spread = ((iota((WIDTH, 256), 0) == (lane // 8) * 4 + lane % 8) & (lane % 8 < 4)).astype(F32).astype(BF16)
-    keys8[...] = nn(ids_b, spread).astype(I32) - 1
-    to_scalar.wait()
-    landed(asks.at[pl.ds(0, COLS - 1)], ask_send)
-    landed(rows_ids.at[pl.ds(0, ROWS - 1)], row_send)
+    to_mine.wait()
+
+    def half(h):
+        return pl.ds(h * WIDTH, WIDTH)
+
+    def give_lin(t, d, tc):
+        for i in range(SLOTS):
+            pull_lin[tc, pl.ds(i, 1)] = lin_b[mine_s[t, tc * SLOTS + i]]
+        send(pull_lin.at[tc], got_lin.at[t, c], plin_send, plin_recv.at[t, d], r, tc, d == 0)
+
+    def give_first(d, _):
+        tc = ahead(d)
+        give_lin(0, d, tc)
+        for i in range(SLOTS):
+            at = mine_s[0, tc * SLOTS + i]
+            for q in range(ROWS):
+                pull[tc * ROWS + q, i] = tab_all[at, q]
+        send(pull.at[pl.ds(tc * ROWS, ROWS)], got.at[c], pull_send, pull_recv.at[d], r, tc, d == 0)
+        return 0
+
+    def give_next(h, d, _):
+        tc = ahead(d)
+        if h == 1:
+            give_lin(1, d, tc)
+        for q in range(ROWS):
+            tr = (r + q) % ROWS
+            place = tr * COLS + tc
+            for i in range(SLOTS):
+                pull_next[h, place, i] = tab_b[h, ids_s[tr * STEPS + 1, tc * SLOTS + i]]
+            send(
+                pull_next.at[h, place], got_next.at[h, c, r], next_send.at[h], pull_recv.at[COLS + h * COLS + d],
+                tr, tc, (d == 0) & (q == 0),
+            )
+        return 0
 
     for t in range(STEPS):
-        if t > 0:
-            landed(pull.at[pl.ds(0, PEERS - 1)], pull_send)
-            landed(pull_lin.at[pl.ds(0, COLS - 1)], plin_send)
-
-        def give(d, _):
-            tc = ahead(d)
-            for i in range(SLOTS):
-                pull_lin[tc, pl.ds(i, 1)] = lin_b[ids_s[r * STEPS + t, tc * SLOTS + i]]
-            pull_lin[tc, pl.ds(4, 4)] = jnp.zeros((4, WIDTH), F32)
-            send(pull_lin.at[tc], got_lin.at[t, c], plin_send, plin_recv.at[t, d], r, tc, d == 0)
-            for q in range(ROWS):
-                tr = (r + q) % ROWS
-                place = tr * COLS + tc
-                for i in range(SLOTS):
-                    pull[place, i] = tab_b[ids_s[tr * STEPS + t, tc * SLOTS + i]]
-                send(
-                    pull.at[place], got.at[t, c, r], pull_send, pull_recv.at[t, d],
-                    tr, tc, (d == 0) & (q == 0),
-                )
-            return 0
-
-        lax.fori_loop(0, COLS, give, 0)
-
-        v = (v0, v1)[t]
         if t == 0:
+            lax.fori_loop(0, COLS, give_first, 0)
+
+        if t == 0:
+            quarter(tab_n, tab_0)
+            tab_f[...] = tab_0[...]
             bring_acc.wait()
             quarter(acc_n, acc_f)
+            for dq in range(1, ROWS):
+                landed(rows_ids.at[(r + 4 - dq) % ROWS], row_recv.at[dq])
+            ids = rows_ids[...].reshape(ROWS * STEPS, WIDTH)
+            ids_v[...] = ids
+            to_scalar = pltpu.make_async_copy(ids_v, ids_s, ids_sem)
+            to_scalar.start()
+            ids_b = ids.astype(F32).astype(BF16)
+            for part in range(4):
+                lane = iota((WIDTH, 512), 1) + part * 512
+                spread = (iota((WIDTH, 512), 0) == behind(lane // 64) * 4 + (lane // 16) % 4).astype(F32).astype(BF16)
+                found = nn(ids_b, spread).astype(I32)
+                keys[:, part * 512 : (part + 1) * 512] = (found - 1) * 16 + iota((8, 512), 1) % 16
+            to_scalar.wait()
+            landed(asks.at[pl.ds(0, COLS - 1)], ask_send)
+            landed(rows_ids.at[pl.ds(0, ROWS - 1)], row_send)
+        v = (v0, v1)[t]
         landed(v, v_sem.at[t])
         stats[...] = jnp.zeros_like(stats)
 
@@ -182,7 +214,9 @@
             return v[holder[t, o * SLOTS + i]]
 
         def tile_of(o, i):
-            quarters = [got[t, o, q, i] for q in range(ROWS)]
+            if t > 0:
+                return jnp.concatenate([got_next[h, o, q, i] for q in range(ROWS) for h in range(2)], axis=0)
+            quarters = [got[o, q, i] for q in range(ROWS)]
             return jnp.concatenate(
                 [quarters[q][:, h * WIDTH : (h + 1) * WIDTH] for q in range(ROWS) for h in range(2)], axis=0
             )
@@ -190,7 +224,11 @@
         def use(d, _):
             o = behind(d)
             landed(got_lin.at[t, o], plin_recv.at[t, d])
-            landed(got.at[t, o], pull_recv.at[t, d])
+            if t == 0:
+                landed(got.at[o], pull_recv.at[d])
+            else:
+                for h in range(2):
+                    landed(got_next.at[h, o], pull_recv.at[COLS + h * COLS + d])
             blocks = [block_of(o, i) for i in range(SLOTS)]
             tiles = [tile_of(o, i) for i in range(SLOTS)]
             stats[:, :WIDTH] += nt(jnp.concatenate(blocks, axis=1), jnp.concatenate(tiles, axis=1))
@@ -260,7 +298,8 @@
         logit_out[pl.ds(t, 1)] = turned[192:193] + turned[224:225] + turned[240:241]
 
         if t > 0:
-            landed(gs.at[pl.ds(0, PEERS - 1)], push_send)
+            for h in range(2):
+                landed(gs.at[h, pl.ds(0, PEERS - 1)], push_send.at[h])
             landed(gls.at[pl.ds(0, COLS - 1)], glin_send)
 
         def grads(d, _):
@@ -277,56 +316,67 @@
                 for q in range(ROWS):
                     for h in range(2):
                         at = 32 * q + 16 * h
-                        gs[q * COLS + o, i, :, pl.ds(h * WIDTH, WIDTH)] = tile[at : at + 16]
-            gls[o] = jnp.concatenate(lins + [jnp.zeros((4, WIDTH), F32)], axis=0)
+                        gs[h, q * COLS + o, i] = tile[at : at + 16]
+            gls[o] = jnp.concatenate(lins, axis=0)
             send(gls.at[o], rl.at[t, c], glin_send, glin_recv.at[t], r, o, d == 0)
+            push(0, d, 0)
+            return 0
+
+        def push(h, d, _):
+            o = ahead(d)
             for dq in range(ROWS):
                 q = (r + dq) % ROWS
                 send(
-                    gs.at[q * COLS + o], rp.at[t, dq * COLS + d], push_send, push_recv.at[t, (d // 4) * 4 + dq],
-                    q, o, (d == 0) & (dq == 0),
+                    gs.at[h, q * COLS + o], rp.at[t, h, dq * COLS + d],
+                    push_send.at[h], push_recv.at[t, h * 32 + (d // 4) * 4 + dq], q, o, (d == 0) & (dq == 0),
                 )
             return 0
 
         lax.fori_loop(0, COLS, grads, 0)
+        lax.fori_loop(0, COLS, functools.partial(push, 1), 0)
 
         dense[...] = jnp.zeros_like(dense)
 
-        def add(n, _):
+        def add(h, n, _):
             g, dq = n // 4, n % 4
             rs = (r + 4 - dq) % 4
             at = dq * COLS + g * 4
-            landed(rp.at[t, pl.ds(at, 4)], push_recv.at[t, n])
+            landed(rp.at[t, h, pl.ds(at, 4)], push_recv.at[t, h * 32 + n])
             keyed = keys[pl.ds(rs * STEPS + t, 1), pl.ds(pl.multiple_of(g * 256, 256), 256)]
             onehot = (iota((512, 256), 0) == jnp.broadcast_to(keyed, (512, 256))).astype(F32).astype(BF16)
-            dense[...] += nn(onehot, rp[t, pl.ds(at, 4)].reshape(256, 256))
-            return 0
-
-        lax.fori_loop(0, 28, add, 0)
+            dense[:, half(h)] += nn(onehot, rp[t, h, pl.ds(at, 4)].reshape(256, WIDTH))
+            return 0
+
+        def update(h):
+            grad = dense[:, half(h)]
+            acc = acc_f[:, half(h)] + grad * grad
+            acc_f[:, half(h)] = acc
+            new = tab_f[:, half(h)] - learn_rate * grad / jnp.sqrt(acc)
+            tab_f[:, half(h)] = new
+            if t < STEPS - 1:
+                tab_b[h, pl.ds(1, BLOCKS)] = new.astype(BF16).reshape(BLOCKS, 16, WIDTH)
+                lax.fori_loop(0, COLS, functools.partial(give_next, h), 0)
+            else:
+                last[h] = (tab_0[:, half(h)] - new).astype(BF16)
+                for dq in range(ROWS):
+                    q = (r + dq) % ROWS
+                    send(last.at[h], back.at[h, r], out_send.at[h], out_recv.at[h], q, c, dq == 0)
+
+        lax.fori_loop(0, 28, functools.partial(add, 0), 0)
         landed(rl.at[t], glin_recv.at[t])
-        keyed = jnp.broadcast_to(keys8[pl.ds(r * STEPS + t, 1)], (BLOCKS, 256))
-        onehot = (iota((BLOCKS, 256), 0) == keyed).astype(F32).astype(BF16)
+        keyed = jnp.broadcast_to(ids_v[pl.ds(r * STEPS + t, 1)] - 1, (BLOCKS, WIDTH))
+        onehot = (iota((BLOCKS, WIDTH), 0) == keyed).astype(F32).astype(BF16)
         if t > 0:
             landed(lin_got.at[t, pl.ds(0, ROWS - 1)], sum_send)
-        lin_part[...] = nn(onehot, rl[t].reshape(COLS * 8, WIDTH).astype(BF16))
+        lin_part[...] = nn(onehot, rl[t].reshape(COLS * SLOTS, WIDTH).astype(BF16))
         for dq in range(ROWS):
             q = (r + dq) % ROWS
             send(lin_part, lin_got.at[t, r], sum_send, sum_recv.at[t], q, c, dq == 0)
 
-        lax.fori_loop(28, 32, add, 0)
-
-        grad = dense[...]
-        acc = acc_f[...] + grad * grad
-        acc_f[...] = acc
-        new = tab_f[...] - learn_rate * grad / jnp.sqrt(acc)
-        tab_f[...] = new
+        lax.fori_loop(28, 32, functools.partial(add, 0), 0)
         if t < STEPS - 1:
-            tab_b[pl.ds(1, BLOCKS)] = new.astype(BF16).reshape(BLOCKS, 16, 256)
-        else:
-            last[...] = (tab_0[...] - new).astype(BF16)
-            for dq in range(ROWS):
-                q = (r + dq) % ROWS
-                send(last, back.at[r], out_send, out_recv, q, c, dq == 0)
+            landed(pull_lin.at[pl.ds(0, COLS - 1)], plin_send)
+        update(0)
 
         landed(lin_got.at[t], sum_recv.at[t])
         grad = lin_got[t, 0] + lin_got[t, 1] + lin_got[t, 2] + lin_got[t, 3]
@@ -336,27 +386,32 @@
         lin_f[...] = new
         lin_b[pl.ds(1, BLOCKS)] = new.reshape(BLOCKS, 1, WIDTH)
 
+        lax.fori_loop(0, 32, functools.partial(add, 1), 0)
+        update(1)
+
     lin_out[...] = lin_f[...]
-    landed(pull.at[pl.ds(0, PEERS - 1)], pull_send)
+    landed(pull.at[pl.ds(0, PEERS - ROWS)], pull_send)
+    for h in range(2):
+        landed(pull_next.at[h, pl.ds(0, PEERS - 1)], next_send.at[h])
+        landed(gs.at[h, pl.ds(0, PEERS - 1)], push_send.at[h])
+        landed(back.at[h], out_recv.at[h])
     landed(pull_lin.at[pl.ds(0, COLS - 1)], plin_send)
     landed(xs.at[pl.ds(0, COLS - 1)], x_send)
     landed(wr.at[0, pl.ds(0, COLS - 1)], w_send)
-    landed(gs.at[pl.ds(0, PEERS - 1)], push_send)
     landed(gls.at[pl.ds(0, COLS - 1)], glin_send)
     landed(lin_got.at[0, pl.ds(0, ROWS - 1)], sum_send)
-    landed(back, out_recv)
-    eye = (iota((WIDTH, WIDTH), 0) == iota((WIDTH, WIDTH), 1)).astype(F32).astype(BF16)
 
     def back_turn(b, _):
         at = pl.ds(pl.multiple_of(b * 16, 16), 16)
         tile = jnp.concatenate(
-            [back[q, at, h * WIDTH : (h + 1) * WIDTH] for q in range(ROWS) for h in range(2)], axis=0
+            [back[h, q, at] for q in range(ROWS) for h in range(2)], axis=0
         )
         delta_out[b] = nt(eye, tile).astype(BF16)
         return 0
 
     lax.fori_loop(0, BLOCKS, back_turn, 0)
-    landed(back.at[pl.ds(0, ROWS - 1)], out_send)
+    for h in range(2):
+        landed(back.at[h, pl.ds(0, ROWS - 1)], out_send.at[h])
 
 
 def list_slots(lists):
@@ -400,46 +455,50 @@
             V((ROWS, STEPS, WIDTH), I32),
             V((8, WIDTH), I32),
             pltpu.SMEM((8, WIDTH), I32),
+            V((STEPS, WIDTH), I32),
+            pltpu.SMEM((STEPS, WIDTH), I32),
             V((8, 2048), I32),
-            V((8, 256), I32),
+            V((BLOCKS + 1, ROWS, 16, 256), BF16),
             V((512, 256), F32),
             V((512, 256), F32),
             V((512, 256), F32),
             V((BLOCKS, WIDTH), F32),
             V((BLOCKS, WIDTH), F32),
-            V((BLOCKS + 1, 16, 256), BF16),
+            V((2, BLOCKS + 1, 16, WIDTH), BF16),
             V((BLOCKS + 1, 1, WIDTH), F32),
             V((PEERS, SLOTS, 16, 256), BF16),
-            V((COLS, 8, WIDTH), F32),
-            V((STEPS, COLS, ROWS, SLOTS, 16, 256), BF16),
-            V((STEPS, COLS, 8, WIDTH), F32),
+            V((COLS, SLOTS, WIDTH), F32),
+            V((COLS, ROWS, SLOTS, 16, 256), BF16),
+            V((STEPS, COLS, SLOTS, WIDTH), F32),
+            V((2, COLS, ROWS, SLOTS, 16, WIDTH), BF16),
+            V((2, PEERS, SLOTS, 16, WIDTH), BF16),
             V((EX, 256), F32),
             V((COLS, 24, WIDTH), F32),
             V((STEPS, COLS, 24, WIDTH), F32),
             V((PART, 256), BF16),
             V((STEPS, COLS, PART, 256), BF16),
             V((256, EX), BF16),
-            V((PEERS, SLOTS, 16, 256), BF16),
-            V((COLS, 8, WIDTH), F32),
-            V((STEPS, PEERS, SLOTS, 16, 256), BF16),
-            V((STEPS, COLS, 8, WIDTH), F32),
+            V((2, PEERS, SLOTS, 16, WIDTH), BF16),
+            V((COLS, SLOTS, WIDTH), F32),
+            V((STEPS, 2, PEERS, SLOTS, 16, WIDTH), BF16),
+            V((STEPS, COLS, SLOTS, WIDTH), F32),
             V((512, 256), F32),
             V((BLOCKS, WIDTH), F32),
             V((STEPS, ROWS, BLOCKS, WIDTH), F32),
-            V((512, 256), BF16),
-            V((ROWS, 512, 256), BF16),
+            V((2, 512, WIDTH), BF16),
+            V((2, ROWS, 512, WIDTH), BF16),
             dma((STEPS,)),
             dma, dma,
             dma, dma,
-            dma, dma((ROWS,)), dma,
-            dma, dma((STEPS, COLS)),
+            dma, dma, dma((ROWS,)), dma,
+            dma, dma((2,)), dma((3 * COLS,)),
             dma, dma((STEPS, COLS)),
             dma, dma((STEPS,)),
             dma, dma((STEPS,)),
-            dma, dma((STEPS, 32)),
+            dma((2,)), dma((STEPS, 64)),
             dma, dma((STEPS,)),
             dma, dma((STEPS,)),
-            dma, dma,
+            dma((2,)), dma((2,)),
         ],
         compiler_params=pltpu.CompilerParams(has_side_effects=True, vmem_limit_bytes=60 * 2**20),
     )(holder, wanted, labels, lin, lin_acc, table, table_acc, values)

time: 298 us -> 288 us (0.966)
  Pallas kernels: 289 us -> 280 us
    pallas_call x1, Pallas kernels: 289 us -> 280 us  [local(): pl.pallas_call(kernel, out_shape=(jax.ShapeDtypeStruct((BLOCKS, WIDTH, WI...]
where the time goes in v3:
time: 288 us
  Pallas kernels  280 us (97%)
  other arithmetic  5.82 us (2%)
    pallas_call x1, Pallas kernels, local(): pl.pallas_call(kernel, out_shape=(jax.ShapeDtypeStruct((BLOCKS, WIDTH, WI...  280 us

profile of v3, /device:TPU:1, one launch (start us, length us, event | category | flops | bytes accessed | tf_op | source)
XLA Modules:
  0.0 288.1 jit_solution(16770458866206883560)
XLA Ops:
  0.6 0.7 fusion.1
  1.3 0.2 convert_reduce_fusion
  1.5 0.7 add_select_fusion
  2.2 0.7 select_reduce_fusion
  2.9 0.1 tile.10
  3.0 0.1 copy.12
  3.1 0.1 copy.13
  3.2 0.6 select_bitcast_fusion.wanted
  3.8 0.0 copy-start
  3.8 280.1 %shard_map.94 = (bf16[32,128,128]{2,1,0:T(8,128)(2,1)}, f32[32,128]{1,0:T(8,128)}, f32[2,512]{1,0:T(2,128)}) custom-call(s32[2,128]{1,0:T(2,128)} %get-tuple-element.10.holder, s32[32,2,128]{2,1,0:T(2,128)} %select_bitcast_fusion.wanted, s32[2,512]{1,0:T(2,128)} %labels.1, f32[32,128]{1,0:T(8,128)} %lin.1, f32[32,128]{1,0:T(8,128)} %lin_acc.1, ...), custom_call_target="tpu_custom_call" | custom-call | tf_op jit(solution)/shard_map/pallas_call | solution.py:440
  283.9 0.0 copy-done
  283.9 0.0 copy-start.1
  284.0 0.0 copy-start.2
  284.0 2.9 %convert_subtract_fusion = f32[32,128,128]{2,1,0:T(8,128)} fusion(f32[32,128,128]{2,1,0:T(8,128)S(1)} %copy-done, bf16[32,128,128]{2,1,0:T(8,128)(2,1)} %get-tuple-element.6), kind=kLoop, calls=%fused_computation | loop fusion | flops 1048576 | bytes 5242880 | tf_op jit(solution)/shard_map/sub | solution.py:505
  286.9 0.0 copy-done.1
  286.9 0.6 copy.16
  287.5 0.0 copy-done.2
  287.5 0.6 copy.17
  (3 shorter events, 0.0 us)
Async XLA Ops:
  3.8 280.1 %copy-start = (f32[32,128,128]{2,1,0:T(8,128)S(1)}, f32[32,128,128]{2,1,0:T(8,128)}, u32[]{:S(2)}) copy-start(f32[32,128,128]{2,1,0:T(8,128)} %table.1) | copy-start | bytes 6291460
  283.9 2.9 %copy-start.1 = (f32[32,128]{1,0:T(8,128)S(1)}, f32[32,128]{1,0:T(8,128)}, u32[]{:S(2)}) copy-start(f32[32,128]{1,0:T(8,128)} %get-tuple-element.17) | copy-start | bytes 49156
  284.0 3.5 %copy-start.2 = (f32[2,512]{1,0:T(2,128)S(1)}, f32[2,512]{1,0:T(2,128)}, u32[]{:S(2)}) copy-start(f32[2,512]{1,0:T(2,128)} %get-tuple-element.18) | copy-start | bytes 12292

commit v4 on v3

--- a/solution.py
+++ b/solution.py
@@ -49,11 +49,14 @@
 
     def ahead(d):
         dz, dy, dk = offsets(d)
-        return ((z + dz) % 4) * 8 + ((y + dy) % 4) * 2 + (k + dk) % 2
+        ez, ey = dz + k * (dy - dz), dy + k * (dz - dy)
+        return ((z + ez) % 4) * 8 + ((y + ey) % 4) * 2 + (k + dk) % 2
 
     def behind(d):
         dz, dy, dk = offsets(d)
-        return ((z + 4 - dz) % 4) * 8 + ((y + 4 - dy) % 4) * 2 + (k + dk) % 2
+        ks = (k + dk) % 2
+        ez, ey = dz + ks * (dy - dz), dy + ks * (dz - dy)
+        return ((z + 4 - ez) % 4) * 8 + ((y + 4 - ey) % 4) * 2 + ks
 
     def send(src, dst, send_sem, recv_sem, row, col, home):
         @pl.when(home)

time: 288 us -> 284 us (0.986)
  Pallas kernels: 280 us -> 276 us
    pallas_call x1, Pallas kernels: 280 us -> 276 us  [local(): pl.pallas_call(kernel, out_shape=(jax.ShapeDtypeStruct((BLOCKS, WIDTH, WI...]
where the time goes in v4:
time: 284 us
  Pallas kernels  276 us (97%)
  other arithmetic  5.82 us (2%)
    pallas_call x1, Pallas kernels, local(): pl.pallas_call(kernel, out_shape=(jax.ShapeDtypeStruct((BLOCKS, WIDTH, WI...  276 us

profile of v4, /device:TPU:1, one launch (start us, length us, event | category | flops | bytes accessed | tf_op | source)
XLA Modules:
  0.0 283.5 jit_solution(8738354940026913349)
XLA Ops:
  0.6 0.7 fusion.1
  1.3 0.2 convert_reduce_fusion
  1.5 0.7 add_select_fusion
  2.2 0.7 select_reduce_fusion
  2.9 0.1 tile.10
  3.0 0.1 copy.12
  3.1 0.1 copy.13
  3.2 0.6 select_bitcast_fusion.wanted
  3.8 0.0 copy-start
  3.8 275.5 %shard_map.94 = (bf16[32,128,128]{2,1,0:T(8,128)(2,1)}, f32[32,128]{1,0:T(8,128)}, f32[2,512]{1,0:T(2,128)}) custom-call(s32[2,128]{1,0:T(2,128)} %get-tuple-element.10.holder, s32[32,2,128]{2,1,0:T(2,128)} %select_bitcast_fusion.wanted, s32[2,512]{1,0:T(2,128)} %labels.1, f32[32,128]{1,0:T(8,128)} %lin.1, f32[32,128]{1,0:T(8,128)} %lin_acc.1, ...), custom_call_target="tpu_custom_call" | custom-call | tf_op jit(solution)/shard_map/pallas_call | solution.py:443
  279.4 0.0 copy-done
  279.4 0.0 copy-start.1
  279.4 0.0 copy-start.2
  279.4 2.9 %convert_subtract_fusion = f32[32,128,128]{2,1,0:T(8,128)} fusion(f32[32,128,128]{2,1,0:T(8,128)S(1)} %copy-done, bf16[32,128,128]{2,1,0:T(8,128)(2,1)} %get-tuple-element.6), kind=kLoop, calls=%fused_computation | loop fusion | flops 1048576 | bytes 5242880 | tf_op jit(solution)/shard_map/sub | solution.py:508
  282.3 0.0 copy-done.1
  282.3 0.6 copy.16
  282.9 0.0 copy-done.2
  282.9 0.6 copy.17
  (3 shorter events, 0.0 us)
Async XLA Ops:
  3.8 275.6 %copy-start = (f32[32,128,128]{2,1,0:T(8,128)S(1)}, f32[32,128,128]{2,1,0:T(8,128)}, u32[]{:S(2)}) copy-start(f32[32,128,128]{2,1,0:T(8,128)} %table.1) | copy-start | bytes 6291460
  279.4 2.9 %copy-start.1 = (f32[32,128]{1,0:T(8,128)S(1)}, f32[32,128]{1,0:T(8,128)}, u32[]{:S(2)}) copy-start(f32[32,128]{1,0:T(8,128)} %get-tuple-element.17) | copy-start | bytes 49156
  279.4 3.5 %copy-start.2 = (f32[2,512]{1,0:T(2,128)S(1)}, f32[2,512]{1,0:T(2,128)}, u32[]{:S(2)}) copy-start(f32[2,512]{1,0:T(2,128)} %get-tuple-element.18) | copy-start | bytes 12292

commit v5 on v4

--- a/solution.py
+++ b/solution.py
@@ -404,15 +404,15 @@
     landed(gls.at[pl.ds(0, COLS - 1)], glin_send)
     landed(lin_got.at[0, pl.ds(0, ROWS - 1)], sum_send)
 
-    def back_turn(b, _):
-        at = pl.ds(pl.multiple_of(b * 16, 16), 16)
-        tile = jnp.concatenate(
-            [back[h, q, at] for q in range(ROWS) for h in range(2)], axis=0
-        )
-        delta_out[b] = nt(eye, tile).astype(BF16)
+    def back_turn(n, _):
+        for i in range(8):
+            b = n * 8 + i
+            at = pl.ds(pl.multiple_of(b * 16, 16), 16)
+            tile = jnp.concatenate([back[h, q, at] for q in range(ROWS) for h in range(2)], axis=0)
+            delta_out[b] = nt(eye, tile).astype(BF16)
         return 0
 
-    lax.fori_loop(0, BLOCKS, back_turn, 0)
+    lax.fori_loop(0, BLOCKS // 8, back_turn, 0)
     for h in range(2):
         landed(back.at[h, pl.ds(0, ROWS - 1)], out_send.at[h])
 

time: 284 us -> 281 us (0.989)
  Pallas kernels: 276 us -> 272 us
    pallas_call x1, Pallas kernels: 276 us -> 272 us  [local(): pl.pallas_call(kernel, out_shape=(jax.ShapeDtypeStruct((BLOCKS, WIDTH, WI...]
where the time goes in v5:
time: 281 us; the launch traced here: 280 us
  Pallas kernels  272 us (97%)
  other arithmetic  5.82 us (2%)
    pallas_call x1, Pallas kernels, local(): pl.pallas_call(kernel, out_shape=(jax.ShapeDtypeStruct((BLOCKS, WIDTH, WI...  272 us

profile of v5, /device:TPU:1, one launch (start us, length us, event | category | flops | bytes accessed | tf_op | source)
XLA Modules:
  0.0 279.8 jit_solution(451905041233326627)
XLA Ops:
  0.6 0.7 fusion.1
  1.3 0.2 convert_reduce_fusion
  1.5 0.7 add_select_fusion
  2.2 0.7 select_reduce_fusion
  2.9 0.1 tile.10
  3.0 0.1 copy.12
  3.1 0.1 copy.13
  3.2 0.6 select_bitcast_fusion.wanted
  3.8 0.0 copy-start
  3.8 271.8 %shard_map.94 = (bf16[32,128,128]{2,1,0:T(8,128)(2,1)}, f32[32,128]{1,0:T(8,128)}, f32[2,512]{1,0:T(2,128)}) custom-call(s32[2,128]{1,0:T(2,128)} %get-tuple-element.10.holder, s32[32,2,128]{2,1,0:T(2,128)} %select_bitcast_fusion.wanted, s32[2,512]{1,0:T(2,128)} %labels.1, f32[32,128]{1,0:T(8,128)} %lin.1, f32[32,128]{1,0:T(8,128)} %lin_acc.1, ...), custom_call_target="tpu_custom_call" | custom-call | tf_op jit(solution)/shard_map/pallas_call | solution.py:443
  275.6 0.0 copy-done
  275.6 0.0 copy-start.1
  275.6 0.0 copy-start.2
  275.6 2.9 %convert_subtract_fusion = f32[32,128,128]{2,1,0:T(8,128)} fusion(f32[32,128,128]{2,1,0:T(8,128)S(1)} %copy-done, bf16[32,128,128]{2,1,0:T(8,128)(2,1)} %get-tuple-element.6), kind=kLoop, calls=%fused_computation | loop fusion | flops 1048576 | bytes 5242880 | tf_op jit(solution)/shard_map/sub | solution.py:508
  278.6 0.0 copy-done.1
  278.6 0.6 copy.16
  279.2 0.0 copy-done.2
  279.2 0.6 copy.17
  (3 shorter events, 0.0 us)
Async XLA Ops:
  3.8 271.8 %copy-start = (f32[32,128,128]{2,1,0:T(8,128)S(1)}, f32[32,128,128]{2,1,0:T(8,128)}, u32[]{:S(2)}) copy-start(f32[32,128,128]{2,1,0:T(8,128)} %table.1) | copy-start | bytes 6291460
  275.6 2.9 %copy-start.1 = (f32[32,128]{1,0:T(8,128)S(1)}, f32[32,128]{1,0:T(8,128)}, u32[]{:S(2)}) copy-start(f32[32,128]{1,0:T(8,128)} %get-tuple-element.17) | copy-start | bytes 49156
  275.6 3.5 %copy-start.2 = (f32[2,512]{1,0:T(2,128)S(1)}, f32[2,512]{1,0:T(2,128)}, u32[]{:S(2)}) copy-start(f32[2,512]{1,0:T(2,128)} %get-tuple-element.18) | copy-start | bytes 12292
